TPU v7x, 512 devices: a whole 4x4x16 slice. The times are simulated.
512 devices in a mesh: row: 4 (over x), col: 16 (over z_hi, y), depth: 8 (over z_lo, core).
Axes of the slice: x: 4, y: 4, z: 16 (z_hi: 4, z_lo: 4; z = z_hi * 4 + z_lo), core: 2. Of those that a mesh axis runs over, the one named last changes fastest.
Arguments:
- integrals: bfloat16 [800, 800, 512], P('col', 'depth', 'row'), may hold values from -0.15625 to 0.15625
- amplitudes: bfloat16 [16, 800, 3200], P('col', ('depth', 'row')), may hold values from -6 to 6
- a_offsets: int32 [9], replicated, may hold values from 0 to 32, as said below
- vir_offsets: int32 [9], replicated, may hold values from 0 to 800, as said below
- c_offsets: int32 [9], replicated, may hold values from 0 to 16, as said below
Outputs:
- ladder: bfloat16 [32, 800, 3200], P(('row', 'depth'), 'col')
Inputs may be any that keep to these rules, and one draw needn't show every extreme that they name: `a_offsets`: offsets of the 8 irrep blocks of the a orbitals: the first is 0, the last is 32, non-decreasing; block k holds irrep k and has at least one orbital. `vir_offsets`: offsets of the 8 irrep blocks of the virtual orbitals: the first is 0, the last is 800, non-decreasing; block k holds irrep k and has at least one orbital. `c_offsets`: offsets of the 8 irrep blocks of the slab's c orbitals: the first is 0, the last is 16, non-decreasing; block k holds irrep k and has at least one orbital.
All inputs are finite; a program needn't handle non-finite values.
Results may differ from a plain program's by a relative error of at most 0.017.
Values may be sent and summed in bfloat16 or wider, within the bound.
No kernel may reach another device: no remote copies, remote signals or barrier semaphores. Data moves between devices by JAX's collectives and lax.ppermute only.
A program may use at most 64 MiB of HBM per device.

v0:
```python
import jax
import jax.numpy as jnp
from jax import lax
from jax.sharding import PartitionSpec as P

CB = 16


def labels_from(offsets, start, count):
    index = start + jnp.arange(count, dtype=jnp.int32)
    above = (index[:, None] >= offsets[None, 1:8]).astype(jnp.int32)
    return jnp.sum(above, axis=1)


def shards(integrals, amplitudes, a_offsets, vir_offsets, c_offsets):
    b_dev, d_dev, merged = integrals.shape
    c_count = CB
    a_dev = merged // c_count
    b_labels = labels_from(vir_offsets, lax.axis_index("col") * b_dev, b_dev)
    d_labels = labels_from(vir_offsets, lax.axis_index("depth") * d_dev, d_dev)
    a_labels = labels_from(a_offsets, lax.axis_index("row") * a_dev, a_dev)
    c_labels = labels_from(c_offsets, jnp.int32(0), c_count)
    four = integrals.reshape(b_dev, d_dev, a_dev, c_count)
    product = jnp.bitwise_xor(
        jnp.bitwise_xor(b_labels[:, None, None, None], d_labels[None, :, None, None]),
        jnp.bitwise_xor(a_labels[None, None, :, None], c_labels[None, None, None, :]),
    )
    masked = jnp.where(product == 0, four, jnp.zeros_like(four))
    local_amps = lax.all_gather(amplitudes, "row", axis=1, tiled=True)
    folded = jnp.einsum(
        "bdac,cdk->abk",
        masked,
        lax.all_gather(local_amps, "col", axis=0, tiled=True),
        preferred_element_type=jnp.float32,
    )
    rounded = folded.astype(jnp.bfloat16).astype(jnp.float32)
    reduced = lax.psum_scatter(
        rounded.astype(jnp.bfloat16), "depth", scatter_dimension=0, tiled=True
    )
    return reduced


def solution(mesh):
    in_specs = (P("col", "depth", "row"), P("col", ("depth", "row"), None), P(), P(), P())
    out_specs = P(("row", "depth"), "col", None)
    return jax.shard_map(shards, mesh=mesh, in_specs=in_specs, out_specs=out_specs, check_vma=False)
```

profile of v0, /device:TPU:1, one launch (start us, length us, event | category | flops | bytes accessed | tf_op | source)
XLA Modules:
  0.0 358.0 jit_solution(15978651435340412209)
XLA Ops:
  6.5 0.0 all-gather.2.cloned.1.call-start
  6.6 1.3 copy.17
  7.9 14.5 %all_gather.6 = bf16[1,100,3200]{2,0,1:T(2,128)(2,1)S(1)} all-gather(bf16[1,25,3200]{2,0,1:T(2,128)(2,1)S(1)} %copy.17), channel_id=1, replica_groups=mesh['row'=4,'col'=16,'depth'=8] {'row'}, dimensions={1}, use_global_device_ids=true | all-gather | bytes 800000 | tf_op jit(solution)/shard_map/all_gather | solution.py:29
  22.3 0.9 copy.18
  23.3 0.0 all-gather.2.cloned.1.call-update
  23.3 0.0 reduce-scatter.5.cloned.1.call-start
  23.4 0.0 copy-done.1
  23.4 0.1 slice.10
  23.4 0.0 copy-done.2
  23.4 0.1 slice.11
  23.5 0.1 slice.12
  23.6 1.0 copy.16
  24.6 0.1 convert_reduce_fusion
  24.7 0.1 convert_reduce_fusion.2
  24.8 0.1 convert_reduce_fusion.3
  24.9 0.2 convert_reduce_fusion.1
  25.0 0.1 broadcast_xor_fusion.1
  25.1 0.1 broadcast_xor_fusion
  25.2 0.7 fusion.11
  25.9 269.2 %all-gather.2.cloned.1.call-done = bf16[16,100,3200]{2,1,0:T(8,128)(2,1)} async-done(((bf16[1,100,3200]{2,1,0:T(8,128)(2,1)}), bf16[16,100,3200]{2,1,0:T(8,128)(2,1)}) %all-gather.2.cloned.1.call-update) | async-done | bytes 10240016 | tf_op jit(solution)/shard_map/all_gather | solution.py:33
  295.1 9.2 %fusion.8 = bf16[8,50,3200]{2,0,1:T(8,128)(2,1)S(1)} fusion(bf16[16,100,3200]{2,1,0:T(8,128)(2,1)} %all-gather.2.cloned.1.call-done, bf16[50,100,8,16]{1,3,2,0:T(8,128)(2,1)S(1)} %fusion.11), kind=kOutput, calls=%fused_computation.4 | convolution fusion | flops 4097280000 | bytes 14080000 | tf_op jit(solution)/shard_map/bdac,cdk->abk/dot_general | solution.py:30
  304.3 1.9 copy.20
  306.2 0.0 reduce-scatter.5.cloned.1.call-update
  306.2 44.9 %reduce-scatter.5.cloned.1.call-done = bf16[1,50,3200]{2,1,0:T(8,128)(2,1)} async-done(((bf16[8,50,3200]{2,1,0:T(8,128)(2,1)}), bf16[1,50,3200]{2,1,0:T(8,128)(2,1)}) %reduce-scatter.5.cloned.1.call-update) | async-done | bytes 320016
  (9 shorter events, 0.0 us)
Async XLA Ops:
  6.5 16.8 %copy-start.1 = (s32[9]{0:T(128)S(1)}, s32[9]{0:T(128)}, u32[]{:S(2)}) copy-start(s32[9]{0:T(128)} %param.8) | copy-start | bytes 112
  6.5 16.9 %copy-start.2 = (s32[9]{0:T(128)S(1)}, s32[9]{0:T(128)}, u32[]{:S(2)}) copy-start(s32[9]{0:T(128)} %param.7) | copy-start | bytes 112
  6.5 17.0 %copy-start.3 = (s32[9]{0:T(128)S(1)}, s32[9]{0:T(128)}, u32[]{:S(2)}) copy-start(s32[9]{0:T(128)} %param.9) | copy-start | bytes 112
  6.5 17.1 %copy-start = (bf16[50,100,128]{2,1,0:T(8,128)(2,1)S(1)}, bf16[50,100,128]{2,1,0:T(8,128)(2,1)}, u32[]{:S(2)}) copy-start(bf16[50,100,128]{2,1,0:T(8,128)(2,1)} %param.5) | copy-start | bytes 3840004
  6.5 288.6 %all-gather.2.cloned.1.call-start = ((), (), s32[]{:S(2)}) async-start(), calls=%async_computation.1 | async-start | bytes 11315200 | tf_op jit(solution)/shard_map/all_gather | solution.py:33
  23.3 327.8 %reduce-scatter.5.cloned.1.call-start = ((), (), s32[]{:S(2)}) async-start(), calls=%async_computation.2 | async-start | bytes 3225600
Sparse Core Ops, SparseCore 0:
  23.4 271.6 all-gather.1
  306.3 44.7 reduce-scatter.4
where the time goes:
time: 360 us; the launch traced here: 358 us
  waiting for transfers between devices  314 us (87%)
  blocking collectives  14.5 us (4%)
  between operations  13.5 us (4%)
  matrix products  9.18 us (3%)
  local copies, waits for them, and re-layouts  5.26 us (1%)
    all_gather x1, waiting for transfers between devices, shards(): lax.all_gather(local_amps, 'col', axis=0, tiled=True)  269 us
    unnamed x3, waiting for transfers between devices  45 us
    all_gather x1, blocking collectives, shards(): local_amps = lax.all_gather(amplitudes, 'row', axis=1, tiled=True)  14.5 us
    dot_general x1, matrix products, shards(): jnp.einsum('bdac,cdk->abk', masked, lax.all_gather(local_amps, 'col', axi...  9.18 us
  transfers between devices with their start and end apart: 2, of which 2 were waited for; matrix products, arithmetic and copies ran while one was open for 1% of the time, Pallas kernels for 0%

commit v1 on v0

v1 whole, which is shorter than its diff:
```python
import jax
import jax.numpy as jnp
from jax import lax
from jax.experimental import pallas as pl
from jax.experimental.pallas import tpu as pltpu
from jax.sharding import Mesh, PartitionSpec as P

CB = 16
A_ROW = 8
B_DEV = 50
D_DEV = 100
RANKS = 9
N_DEV = 800
ROWS = A_ROW * B_DEV
KB = 128


def count_at_or_above(index, offsets):
    total = jnp.zeros_like(index)
    for k in range(1, 8):
        total = total + jnp.where(index >= offsets[k], 1, 0)
    return total


def squeeze_kernel(place, a_off, v_off, c_off, v_ref, w_ref, by_b):
    step = pl.program_id(0)
    b_step = v_ref.shape[0]
    lane = lax.broadcasted_iota(jnp.int32, (D_DEV, KB), 1)
    drow = lax.broadcasted_iota(jnp.int32, (D_DEV, KB), 0)
    base = count_at_or_above(drow + place[1], v_off)
    base = base ^ count_at_or_above((lane >> 4) + place[2], a_off)
    base = base ^ count_at_or_above(lane & 15, c_off)
    elane = lax.broadcasted_iota(jnp.int32, (RANKS * A_ROW, KB), 1)
    erow = lax.broadcasted_iota(jnp.int32, (RANKS * A_ROW, KB), 0)
    c = elane & 15
    c_label = count_at_or_above(c, c_off)
    first = jnp.zeros_like(c)
    for k in range(8):
        first = first + jnp.where(c_label == k, c_off[k], 0)
    pick = ((elane >> 4) == (erow & 7)) & ((c - first) == (erow >> 3))
    pick = jnp.where(pick, 1.0, 0.0).astype(jnp.bfloat16)

    @pl.when(step == 0)
    def _():
        by_b[...] = jnp.zeros_like(by_b)

    b0 = place[0] + step * b_step
    for p in range(b_step // 2):
        halves = []
        for q in range(2):
            b = 2 * p + q
            b_label = count_at_or_above(b0 + b, v_off)
            x = jnp.where(base == b_label, v_ref[b].astype(jnp.float32), 0.0).astype(jnp.bfloat16)
            halves.append(lax.dot_general(pick, x, (((1,), (1,)), ((), ())), preferred_element_type=jnp.float32))
        for r in range(RANKS):
            pair = jnp.concatenate([h[r * A_ROW:(r + 1) * A_ROW] for h in halves], axis=0)
            start = pl.multiple_of(step * (b_step * A_ROW) + 16 * p, 16)
            by_b[r, pl.ds(start, 16), pl.ds(0, D_DEV)] = pair.astype(jnp.bfloat16)

    @pl.when(step == pl.num_programs(0) - 1)
    def _():
        to = lax.broadcasted_iota(jnp.int32, (ROWS, ROWS), 0)
        source = lax.broadcasted_iota(jnp.int32, (ROWS, ROWS), 1)
        a = jnp.zeros_like(to)
        for k in range(1, A_ROW):
            a = a + jnp.where(to >= k * B_DEV, 1, 0)
        move = jnp.where(source == (to - a * B_DEV) * A_ROW + a, 1.0, 0.0).astype(jnp.bfloat16)
        for r in range(RANKS):
            w_ref[r] = jnp.dot(move, by_b[r], preferred_element_type=jnp.float32).astype(jnp.bfloat16)


def squeeze(place, a_off, v_off, c_off, v):
    b_step = 10
    smem = pl.BlockSpec(memory_space=pltpu.SMEM)
    return pl.pallas_call(
        squeeze_kernel,
        grid=(B_DEV // b_step,),
        in_specs=[smem] * 4 + [pl.BlockSpec((b_step, D_DEV, KB), lambda i: (i, 0, 0))],
        out_specs=pl.BlockSpec((RANKS, ROWS, KB), lambda i: (0, 0, 0)),
        out_shape=jax.ShapeDtypeStruct((RANKS, ROWS, KB), jnp.bfloat16),
        scratch_shapes=[pltpu.VMEM((RANKS, ROWS, KB), jnp.bfloat16)],
        compiler_params=pltpu.CompilerParams(vmem_limit_bytes=40 * 2**20),
        cost_estimate=pl.CostEstimate(flops=2 * 5000 * 128 * 72, bytes_accessed=2400000, transcendentals=0),
        name="squeeze",
    )(place, a_off, v_off, c_off, v)


def contract_kernel(place, a_off, v_off, c_off, w_ref, t0, t1, t2, t3, mine_ref, other_ref, tp, lhs, acc, result):
    step = pl.program_id(0)

    @pl.when(step == 0)
    def _():
        tp[...] = jnp.zeros_like(tp)
        for j, t in enumerate((t0, t1, t2, t3)):
            for z in range(4):
                tp[pl.ds((4 * j + z) * KB, D_DEV), :] = t[z]

    row = lax.broadcasted_iota(jnp.int32, (ROWS, KB), 0)
    lane = lax.broadcasted_iota(jnp.int32, (ROWS, KB), 1)
    a = jnp.zeros_like(row)
    for k in range(1, A_ROW):
        a = a + jnp.where(row >= k * B_DEV, 1, 0)
    base = count_at_or_above(row - a * B_DEV + place[0], v_off)
    base = base ^ count_at_or_above(a + step * A_ROW, a_off)
    base = base ^ count_at_or_above(lane + place[1], v_off)
    for j in range(4):
        y = (place[3] + j) & 3
        for z in range(4):
            c = 4 * z + y
            c_label = count_at_or_above(c, c_off)
            rank = c - c_off[c_label]
            w = w_ref[0, rank].astype(jnp.float32)
            lhs[:, pl.ds((4 * j + z) * KB, KB)] = jnp.where(base == c_label, w, 0.0).astype(jnp.bfloat16)
    acc[...] = jnp.dot(lhs[...], tp[...], preferred_element_type=jnp.float32)
    for s in range(4):
        @pl.when(step == s)
        def _():
            for a in range(A_ROW):
                result[a, pl.ds(s * B_DEV, B_DEV), :] = acc[pl.ds(a * B_DEV, B_DEV), :]

    @pl.when(step == 3)
    def _():
        for z in range(4):
            low = result[2 * z].astype(jnp.bfloat16)
            high = result[2 * z + 1].astype(jnp.bfloat16)
            is_low = place[4] == 0
            mine_ref[z] = jnp.where(is_low, low, high)
            other_ref[z] = jnp.where(is_low, high, low)


def contract(place, a_off, v_off, c_off, w, ts):
    smem = pl.BlockSpec(memory_space=pltpu.SMEM)
    t_spec = pl.BlockSpec((4, D_DEV, N_DEV), lambda i: (0, 0, 0))
    o_spec = pl.BlockSpec((4, 4 * B_DEV, N_DEV), lambda i: (0, 0, 0))
    o_shape = jax.ShapeDtypeStruct((4, 4 * B_DEV, N_DEV), jnp.bfloat16)
    return pl.pallas_call(
        contract_kernel,
        grid=(4,),
        in_specs=[smem] * 4 + [pl.BlockSpec((1, RANKS, ROWS, KB), lambda i: (i, 0, 0, 0))] + [t_spec] * 4,
        out_specs=[o_spec, o_spec],
        out_shape=[o_shape, o_shape],
        scratch_shapes=[
            pltpu.VMEM((CB * KB, N_DEV), jnp.bfloat16),
            pltpu.VMEM((ROWS, CB * KB), jnp.bfloat16),
            pltpu.VMEM((ROWS, N_DEV), jnp.float32),
            pltpu.VMEM((A_ROW, 4 * B_DEV, N_DEV), jnp.float32),
        ],
        compiler_params=pltpu.CompilerParams(vmem_limit_bytes=50 * 2**20),
        cost_estimate=pl.CostEstimate(flops=2 * 1600 * 2048 * 800, bytes_accessed=10000000, transcendentals=0),
        name="contract",
    )(place, a_off, v_off, c_off, w, *ts)


def turn(k):
    return [(i, (i + k) % 4) for i in range(4)]


def shards(integrals, amplitudes, a_offsets, vir_offsets, c_offsets):
    zh, y, x = lax.axis_index("zh"), lax.axis_index("y"), lax.axis_index("x")
    zl, core = lax.axis_index("zl"), lax.axis_index("core")
    place = jnp.stack([(zh * 4 + y) * B_DEV, (zl * 2 + core) * D_DEV, x * A_ROW, y, core]).astype(jnp.int32)
    offs = (a_offsets, vir_offsets, c_offsets)
    t = lax.all_to_all(amplitudes.reshape(25, 4, N_DEV), "x", 1, 0, tiled=True).reshape(1, D_DEV, N_DEV)
    w = squeeze(place, *offs, integrals)
    w = lax.all_gather(w, "x", axis=0)
    t = lax.all_gather(t, "zh", axis=0, tiled=True)
    t1, t2, t3 = (lax.ppermute(t, "y", turn(k)) for k in (3, 2, 1))
    mine, other = contract(place, *offs, w, (t, t1, t2, t3))
    got = lax.ppermute(other, "core", [(0, 1), (1, 0)])

    def pair(k):
        which = zl ^ k
        a = lax.dynamic_index_in_dim(mine, which, 0, keepdims=False).astype(jnp.float32)
        b = lax.dynamic_index_in_dim(got, which, 0, keepdims=False).astype(jnp.float32)
        return a + b

    total = pair(0)
    for part in [lax.ppermute(pair(k).astype(jnp.bfloat16), "zl", [(i, i ^ k) for i in range(4)]) for k in (3, 2, 1)]:
        total = total + part.astype(jnp.float32)
    out = lax.all_to_all(total.astype(jnp.bfloat16).reshape(4, B_DEV, N_DEV), "x", 0, 0, tiled=True)
    return out.transpose(1, 0, 2).reshape(1, B_DEV, 4 * N_DEV)


def solution(mesh):
    fine = Mesh(mesh.devices.reshape(4, 4, 4, 4, 2), ("x", "zh", "y", "zl", "core"))
    in_specs = (P(("zh", "y"), ("zl", "core"), "x"), P(("zh", "y"), ("zl", "core", "x"), None), P(), P(), P())
    out_specs = P(("x", "zl", "core"), ("zh", "y"), None)
    return jax.shard_map(shards, mesh=fine, in_specs=in_specs, out_specs=out_specs, check_vma=False)
```

time: 360 us -> 179 us (0.50)
  waiting for transfers between devices: 314 us -> 60.3 us
  blocking collectives: 14.5 us -> 56 us
  starting transfers between devices: 0.08 us -> 22.4 us
  Pallas kernels: 0 us -> 17.4 us
  matrix products: 9.18 us -> 0 us
    all_gather x1, waiting for transfers between devices: 269 us -> 0.02 us  [shards(): w = lax.all_gather(w, 'x', axis=0)]
    ppermute x0 -> x7, waiting for transfers between devices: none -> 60.2 us  [the longest x3 31.7 us: shards(): t1, t2, t3 = (lax.ppermute(t, 'y', turn(k)) for k in (3, 2, 1))]
    unnamed x3 -> x1, waiting for transfers between devices: 45 us -> 0.02 us
    ppermute x0 -> x7, starting transfers between devices: none -> 22.4 us  [the longest x3 10.8 us: shards(): t1, t2, t3 = (lax.ppermute(t, 'y', turn(k)) for k in (3, 2, 1))]
    all_gather x1, blocking collectives: 14.5 us -> 36.4 us  [shards(): t = lax.all_gather(t, 'zh', axis=0, tiled=True)]
    all_to_all x0 -> x2, blocking collectives: none -> 19.6 us  [the longest x1 10 us: shards(): lax.all_to_all(amplitudes.reshape(25, 4, N_DEV), 'x', 1, 0, tiled=True)]
    pallas_call x0 -> x2, Pallas kernels: none -> 17.4 us  [the longest x1 12.7 us: contract(): pl.pallas_call(contract_kernel, grid=(4,), in_specs=[smem] * 4 + [pl.Bloc...]
    dot_general x1 -> x0, matrix products: 9.18 us -> none  [shards(): jnp.einsum('bdac,cdk->abk', masked, lax.all_gather(local_amps, 'col', axi...]
  transfers between devices with their start and end apart: 2 -> 8, of which waited for: 2 -> 6; matrix products, arithmetic and copies ran while one was open for 1% -> 1% of each run, Pallas kernels for 0% -> 0%
where the time goes in v1:
time: 179 us; the launch traced here: 178 us
  waiting for transfers between devices  60.3 us (34%)
  blocking collectives  56 us (31%)
  starting transfers between devices  22.4 us (13%)
  Pallas kernels  17.4 us (10%)
  between operations  13.6 us (8%)
  local copies, waits for them, and re-layouts  5.68 us (3%)
  other arithmetic  2.78 us (2%)
    all_gather x1, blocking collectives, shards(): t = lax.all_gather(t, 'zh', axis=0, tiled=True)  36.4 us
    ppermute x3, waiting for transfers between devices, shards(): t1, t2, t3 = (lax.ppermute(t, 'y', turn(k)) for k in (3, 2, 1))  31.7 us
    ppermute x3, waiting for transfers between devices, shards(): lax.ppermute(pair(k).astype(jnp.bfloat16), 'zl', [(i, i ^ k) for i in ran...  25.6 us
    pallas_call x1, Pallas kernels, contract(): pl.pallas_call(contract_kernel, grid=(4,), in_specs=[smem] * 4 + [pl.Bloc...  12.7 us
    ppermute x3, starting transfers between devices, shards(): t1, t2, t3 = (lax.ppermute(t, 'y', turn(k)) for k in (3, 2, 1))  10.8 us
    all_to_all x1, blocking collectives, shards(): lax.all_to_all(amplitudes.reshape(25, 4, N_DEV), 'x', 1, 0, tiled=True)  10 us
    all_to_all x1, blocking collectives, shards(): lax.all_to_all(total.astype(jnp.bfloat16).reshape(4, B_DEV, N_DEV), 'x',...  9.6 us
    ppermute x3, starting transfers between devices, shards(): lax.ppermute(pair(k).astype(jnp.bfloat16), 'zl', [(i, i ^ k) for i in ran...  9.27 us
  transfers between devices with their start and end apart: 8, of which 6 were waited for; matrix products, arithmetic and copies ran while one was open for 1% of the time, Pallas kernels for 0%

profile of v1, /device:TPU:1, one launch (start us, length us, event | category | flops | bytes accessed | tf_op | source)
XLA Modules:
  0.0 178.1 jit_solution(16543340561355061179)
XLA Ops:
  6.6 1.3 copy-done
  7.9 0.7 copy-done.1
  8.6 0.7 copy-done.3
  9.9 4.7 %squeeze.10 = bf16[9,400,128]{2,1,0:T(8,128)(2,1)} custom-call(s32[5]{0:T(128)S(1)} %stack.23.place, s32[9]{0:T(128)S(1)} %copy-done.1, s32[9]{0:T(128)S(1)} %copy-done.3, s32[9]{0:T(128)S(1)} %copy-done.5, bf16[50,100,128]{2,1,0:T(8,128)(2,1)S(1)} %copy-done), custom_call_target="tpu_custom_call" | custom-call | flops 92160000 | bytes 2400000 | tf_op jit(solution)/shard_map/squeeze/pallas_call | solution.py:75
  15.0 10.0 %all_to_all.20 = bf16[25,4,800]{2,0,1:T(8,128)(2,1)S(1)} all-to-all(bf16[25,4,800]{2,0,1:T(8,128)(2,1)S(1)} %copy.11), channel_id=1, replica_groups=mesh['x'=4,'zh'=4,'y'=4,'zl'=4,'core'=2] {'x'}, dimensions={1} | all-to-all | bytes 320000 | tf_op jit(solution)/shard_map/all_to_all | solution.py:163
  25.1 36.4 %all_gather.11.t0 = bf16[4,100,800]{2,1,0:T(8,128)(2,1)S(1)} all-gather(bf16[1,100,800]{2,1,0:T(8,128)(2,1)S(1)} %reshape.29), channel_id=1, replica_groups=mesh['x'=4,'zh'=4,'y'=4,'zl'=4,'core'=2] {'zh'}, dimensions={0}, use_global_device_ids=true | all-gather | bytes 800000 | tf_op jit(solution)/shard_map/all_gather | solution.py:166
  61.7 5.9 %collective-permute-start = (bf16[4,100,800]{2,0,1:T(4,128)(2,1)S(1)}, bf16[4,100,800]{2,0,1:T(4,128)(2,1)S(1)}, u32[]{:S(2)}, u32[]{:S(2)}) collective-permute-start(bf16[4,100,800]{2,0,1:T(4,128)(2,1)S(1)} %copy.12), channel_id=1, source_target_pairs={{0,24},{8,0},{16,8},{24,16},{1,25},{9,1},{17,9},{25,17},{2,26},{10... | collective-permute-start | bytes 1920008 | tf_op jit(solution)/shard_map/ppermute | solution.py:167
  67.6 2.1 %collective-permute-start.1 = (bf16[4,100,800]{2,0,1:T(4,128)(2,1)S(1)}, bf16[4,100,800]{2,0,1:T(4,128)(2,1)S(1)}, u32[]{:S(2)}, u32[]{:S(2)}) collective-permute-start(bf16[4,100,800]{2,0,1:T(4,128)(2,1)S(1)} %copy.12), channel_id=1, source_target_pairs={{0,16},{8,24},{16,0},{24,8},{1,17},{9,25},{17,1},{25,9},{2,18},{10... | collective-permute-start | bytes 1920008 | tf_op jit(solution)/shard_map/ppermute | solution.py:167
  69.7 2.8 %collective-permute-start.2 = (bf16[4,100,800]{2,0,1:T(4,128)(2,1)S(1)}, bf16[4,100,800]{2,0,1:T(4,128)(2,1)S(1)}, u32[]{:S(2)}, u32[]{:S(2)}) collective-permute-start(bf16[4,100,800]{2,0,1:T(4,128)(2,1)S(1)} %copy.12), channel_id=1, source_target_pairs={{0,8},{8,16},{16,24},{24,0},{1,9},{9,17},{17,25},{25,1},{2,10},{10... | collective-permute-start | bytes 1920008 | tf_op jit(solution)/shard_map/ppermute | solution.py:167
  72.5 11.3 %collective-permute-done = bf16[4,100,800]{2,0,1:T(4,128)(2,1)S(1)} collective-permute-done((bf16[4,100,800]{2,0,1:T(4,128)(2,1)S(1)}, bf16[4,100,800]{2,0,1:T(4,128)(2,1)S(1)}, u32[]{:S(2)}, u32[]{:S(2)}) %collective-permute-start) | collective-permute-done | bytes 640032 | tf_op jit(solution)/shard_map/ppermute | solution.py:167
  83.9 1.0 collective-permute-done.1
  85.0 19.3 %collective-permute-done.2 = bf16[4,100,800]{2,0,1:T(4,128)(2,1)S(1)} collective-permute-done((bf16[4,100,800]{2,0,1:T(4,128)(2,1)S(1)}, bf16[4,100,800]{2,0,1:T(4,128)(2,1)S(1)}, u32[]{:S(2)}, u32[]{:S(2)}) %collective-permute-start.2) | collective-permute-done | bytes 640032 | tf_op jit(solution)/shard_map/ppermute | solution.py:167
  104.5 12.7 %contract.1 = (bf16[4,200,800]{2,1,0:T(8,128)(2,1)}, bf16[4,200,800]{2,1,0:T(8,128)(2,1)}) custom-call(s32[5]{0:T(128)S(1)} %stack.23.place, s32[9]{0:T(128)S(1)} %copy-done.2, s32[9]{0:T(128)S(1)} %copy-done.4, s32[9]{0:T(128)S(1)} %copy-done.6, bf16[4,9,400,128]{3,2,1,0:T(8,128)(2,1)} %bitcast.28, bf16[4,100,800]{2,1,0:T(8,128)(2,1)S(1)} %all_gather.11.t0, ...), custom_call_target="tpu_custom_call" | custom-call | flops 5242880000 | bytes 10000000 | tf_op jit(solution)/shard_map/contract/pallas_call | solution.py:136
  117.2 2.4 %collective-permute-start.3 = (bf16[4,200,800]{2,1,0:T(8,128)(2,1)}, bf16[4,200,800]{2,1,0:T(8,128)(2,1)S(1)}, u32[]{:S(2)}, u32[]{:S(2)}) collective-permute-start(bf16[4,200,800]{2,1,0:T(8,128)(2,1)} %get-tuple-element.8), channel_id=1, source_target_pairs={{0,1},{1,0},{2,3},{3,2},{4,5},{5,4},{6,7},{7,6},{8,9},{9,8},{10,11... | collective-permute-start | bytes 3840008 | tf_op jit(solution)/shard_map/ppermute | solution.py:169
  119.6 3.0 %collective-permute-done.3 = bf16[4,200,800]{2,1,0:T(8,128)(2,1)S(1)} collective-permute-done((bf16[4,200,800]{2,1,0:T(8,128)(2,1)}, bf16[4,200,800]{2,1,0:T(8,128)(2,1)S(1)}, u32[]{:S(2)}, u32[]{:S(2)}) %collective-permute-start.3) | collective-permute-done | bytes 1280032 | tf_op jit(solution)/shard_map/ppermute | solution.py:169
  122.7 1.5 fusion.3
  124.1 2.3 %collective-permute-start.4 = (bf16[200,800]{1,0:T(8,128)(2,1)S(1)}, bf16[200,800]{1,0:T(8,128)(2,1)S(1)}, u32[]{:S(2)}, u32[]{:S(2)}) collective-permute-start(bf16[200,800]{1,0:T(8,128)(2,1)S(1)} %get-tuple-element.9), channel_id=1, source_target_pairs={{0,6},{2,4},{4,2},{6,0},{1,7},{3,5},{5,3},{7,1},{8,14},{10,12},{12... | collective-permute-start | bytes 960008 | tf_op jit(solution)/shard_map/ppermute | solution.py:178
  126.4 3.0 %collective-permute-start.5 = (bf16[200,800]{1,0:T(8,128)(2,1)S(1)}, bf16[200,800]{1,0:T(8,128)(2,1)S(1)}, u32[]{:S(2)}, u32[]{:S(2)}) collective-permute-start(bf16[200,800]{1,0:T(8,128)(2,1)S(1)} %get-tuple-element.11), channel_id=1, source_target_pairs={{0,4},{2,6},{4,0},{6,2},{1,5},{3,7},{5,1},{7,3},{8,12},{10,14},{12... | collective-permute-start | bytes 960008 | tf_op jit(solution)/shard_map/ppermute | solution.py:178
  129.4 4.0 %collective-permute-start.6 = (bf16[200,800]{1,0:T(8,128)(2,1)S(1)}, bf16[200,800]{1,0:T(8,128)(2,1)}, u32[]{:S(2)}, u32[]{:S(2)}) collective-permute-start(bf16[200,800]{1,0:T(8,128)(2,1)S(1)} %get-tuple-element.10), channel_id=1, source_target_pairs={{0,2},{2,0},{4,6},{6,4},{1,3},{3,1},{5,7},{7,5},{8,10},{10,8},{12,... | collective-permute-start | bytes 960008 | tf_op jit(solution)/shard_map/ppermute | solution.py:178
  133.4 4.1 %collective-permute-done.4 = bf16[200,800]{1,0:T(8,128)(2,1)S(1)} collective-permute-done((bf16[200,800]{1,0:T(8,128)(2,1)S(1)}, bf16[200,800]{1,0:T(8,128)(2,1)S(1)}, u32[]{:S(2)}, u32[]{:S(2)}) %collective-permute-start.4) | collective-permute-done | bytes 320032 | tf_op jit(solution)/shard_map/ppermute | solution.py:178
  137.5 21.5 %collective-permute-done.5 = bf16[200,800]{1,0:T(8,128)(2,1)S(1)} collective-permute-done((bf16[200,800]{1,0:T(8,128)(2,1)S(1)}, bf16[200,800]{1,0:T(8,128)(2,1)S(1)}, u32[]{:S(2)}, u32[]{:S(2)}) %collective-permute-start.5) | collective-permute-done | bytes 320032 | tf_op jit(solution)/shard_map/ppermute | solution.py:178
  159.0 1.3 fusion.2
  160.4 9.6 %all_to_all.21 = bf16[4,50,800]{2,1,0:T(8,128)(2,1)S(1)} all-to-all(bf16[4,50,800]{2,1,0:T(8,128)(2,1)S(1)} %reshape.30), channel_id=1, replica_groups=mesh['x'=4,'zh'=4,'y'=4,'zl'=4,'core'=2] {'x'}, dimensions={0} | all-to-all | bytes 640000 | tf_op jit(solution)/shard_map/all_to_all | solution.py:180
  170.2 1.1 reshape.31
  (27 shorter events, 2.0 us)
Async XLA Ops:
  6.5 97.9 %all-gather.3.cloned.1.call-start = ((), (), s32[]{:S(2)}) async-start(), calls=%async_computation.2 | async-start | bytes 4608000 | tf_op jit(solution)/shard_map/all_gather | solution.py:165
  6.6 1.3 copy-start
  7.9 0.7 copy-start.1
  8.6 0.7 copy-start.3
  9.3 0.7 copy-start.5
  9.9 4.7 %copy-start.7 = (bf16[1,25,3200]{2,1,0:T(8,128)(2,1)S(1)}, bf16[1,25,3200]{2,1,0:T(8,128)(2,1)}, u32[]{:S(2)}) copy-start(bf16[1,25,3200]{2,1,0:T(8,128)(2,1)} %param.6) | copy-start | bytes 480004
  61.7 22.0 %collective-permute-start = (bf16[4,100,800]{2,0,1:T(4,128)(2,1)S(1)}, bf16[4,100,800]{2,0,1:T(4,128)(2,1)S(1)}, u32[]{:S(2)}, u32[]{:S(2)}) collective-permute-start(bf16[4,100,800]{2,0,1:T(4,128)(2,1)S(1)} %copy.12), channel_id=1, source_target_pairs={{0,24},{8,0},{16,8},{24,16},{1,25},{9,1},{17,9},{25,17},{2,26},{10... | collective-permute-start | bytes 1920008 | tf_op jit(solution)/shard_map/ppermute | solution.py:167
  67.6 17.3 %collective-permute-start.1 = (bf16[4,100,800]{2,0,1:T(4,128)(2,1)S(1)}, bf16[4,100,800]{2,0,1:T(4,128)(2,1)S(1)}, u32[]{:S(2)}, u32[]{:S(2)}) collective-permute-start(bf16[4,100,800]{2,0,1:T(4,128)(2,1)S(1)} %copy.12), channel_id=1, source_target_pairs={{0,16},{8,24},{16,0},{24,8},{1,17},{9,25},{17,1},{25,9},{2,18},{10... | collective-permute-start | bytes 1920008 | tf_op jit(solution)/shard_map/ppermute | solution.py:167
  69.7 34.6 %collective-permute-start.2 = (bf16[4,100,800]{2,0,1:T(4,128)(2,1)S(1)}, bf16[4,100,800]{2,0,1:T(4,128)(2,1)S(1)}, u32[]{:S(2)}, u32[]{:S(2)}) collective-permute-start(bf16[4,100,800]{2,0,1:T(4,128)(2,1)S(1)} %copy.12), channel_id=1, source_target_pairs={{0,8},{8,16},{16,24},{24,0},{1,9},{9,17},{17,25},{25,1},{2,10},{10... | collective-permute-start | bytes 1920008 | tf_op jit(solution)/shard_map/ppermute | solution.py:167
  83.8 20.6 %copy-start.2 = (s32[9]{0:T(128)S(1)}, s32[9]{0:T(128)}, u32[]{:S(2)}) copy-start(s32[9]{0:T(128)} %a_off.3) | copy-start | bytes 112
  83.9 20.6 %copy-start.4 = (s32[9]{0:T(128)S(1)}, s32[9]{0:T(128)}, u32[]{:S(2)}) copy-start(s32[9]{0:T(128)} %v_off.3) | copy-start | bytes 112
  83.9 20.6 %copy-start.6 = (s32[9]{0:T(128)S(1)}, s32[9]{0:T(128)}, u32[]{:S(2)}) copy-start(s32[9]{0:T(128)} %c_off.3) | copy-start | bytes 112
  117.2 5.4 %collective-permute-start.3 = (bf16[4,200,800]{2,1,0:T(8,128)(2,1)}, bf16[4,200,800]{2,1,0:T(8,128)(2,1)S(1)}, u32[]{:S(2)}, u32[]{:S(2)}) collective-permute-start(bf16[4,200,800]{2,1,0:T(8,128)(2,1)} %get-tuple-element.8), channel_id=1, source_target_pairs={{0,1},{1,0},{2,3},{3,2},{4,5},{5,4},{6,7},{7,6},{8,9},{9,8},{10,11... | collective-permute-start | bytes 3840008 | tf_op jit(solution)/shard_map/ppermute | solution.py:169
  124.1 13.4 %collective-permute-start.4 = (bf16[200,800]{1,0:T(8,128)(2,1)S(1)}, bf16[200,800]{1,0:T(8,128)(2,1)S(1)}, u32[]{:S(2)}, u32[]{:S(2)}) collective-permute-start(bf16[200,800]{1,0:T(8,128)(2,1)S(1)} %get-tuple-element.9), channel_id=1, source_target_pairs={{0,6},{2,4},{4,2},{6,0},{1,7},{3,5},{5,3},{7,1},{8,14},{10,12},{12... | collective-permute-start | bytes 960008 | tf_op jit(solution)/shard_map/ppermute | solution.py:178
  126.4 32.6 %collective-permute-start.5 = (bf16[200,800]{1,0:T(8,128)(2,1)S(1)}, bf16[200,800]{1,0:T(8,128)(2,1)S(1)}, u32[]{:S(2)}, u32[]{:S(2)}) collective-permute-start(bf16[200,800]{1,0:T(8,128)(2,1)S(1)} %get-tuple-element.11), channel_id=1, source_target_pairs={{0,4},{2,6},{4,0},{6,2},{1,5},{3,7},{5,1},{7,3},{8,12},{10,14},{12... | collective-permute-start | bytes 960008 | tf_op jit(solution)/shard_map/ppermute | solution.py:178
  129.4 29.5 %collective-permute-start.6 = (bf16[200,800]{1,0:T(8,128)(2,1)S(1)}, bf16[200,800]{1,0:T(8,128)(2,1)}, u32[]{:S(2)}, u32[]{:S(2)}) collective-permute-start(bf16[200,800]{1,0:T(8,128)(2,1)S(1)} %get-tuple-element.10), channel_id=1, source_target_pairs={{0,2},{2,0},{4,6},{6,4},{1,3},{3,1},{5,7},{7,5},{8,10},{10,8},{12,... | collective-permute-start | bytes 960008 | tf_op jit(solution)/shard_map/ppermute | solution.py:178
Sparse Core Ops, SparseCore 0:
  14.8 56.9 all-gather.2

commit v2 on v0

v2 whole, which is shorter than its diff:
```python
import functools

import jax
import jax.numpy as jnp
from jax import lax
from jax.experimental import pallas as pl
from jax.experimental.pallas import tpu as pltpu
from jax.sharding import Mesh, PartitionSpec as P

CB = 16
A_ROW = 8
B_DEV = 50
D_DEV = 100
N_DEV = 400
GROUPS = 8
ROWS = A_ROW * B_DEV
KB = 128
TILES = N_DEV // KB
LEFT = N_DEV - TILES * KB
PACKED = 160
SWAP = [(0, 1), (1, 0)]
RANKS_MOST = 9
RANKS_FEW = 3


def count_at_or_above(index, offsets):
    total = jnp.zeros_like(index)
    for k in range(1, 8):
        total = total + jnp.where(index >= offsets[k], 1, 0)
    return total


class Part:
    def __init__(self, table, start):
        self.table, self.start = table, start

    def __getitem__(self, k):
        return self.table[self.start + k]


def parts_of(table):
    return Part(table, 0), Part(table, 8), Part(table, 17), Part(table, 26)


def a_of(row):
    a = jnp.zeros_like(row)
    for k in range(1, A_ROW):
        a = a + jnp.where(row >= k * B_DEV, 1, 0)
    return a


def squeeze_kernel(ranks, table, v_ref, w_ref, by_b):
    place, a_off, v_off, c_off = parts_of(table)
    step = pl.program_id(0)
    b_step = v_ref.shape[0]
    lane = lax.broadcasted_iota(jnp.int32, (D_DEV, KB), 1)
    drow = lax.broadcasted_iota(jnp.int32, (D_DEV, KB), 0)
    base = count_at_or_above(drow + place[1], v_off)
    base = base ^ count_at_or_above((lane >> 4) + place[2] * A_ROW, a_off)
    base = base ^ count_at_or_above(lane & 15, c_off)
    elane = lax.broadcasted_iota(jnp.int32, (ranks * A_ROW, KB), 1)
    erow = lax.broadcasted_iota(jnp.int32, (ranks * A_ROW, KB), 0)
    c = elane & 15
    c_label = count_at_or_above(c, c_off)
    first = jnp.zeros_like(c)
    for k in range(8):
        first = first + jnp.where(c_label == k, c_off[k], 0)
    pick = ((elane >> 4) == (erow & 7)) & ((c - first) == (erow >> 3))
    pick = jnp.where(pick, 1.0, 0.0).astype(jnp.bfloat16)

    @pl.when(step == 0)
    def _():
        by_b[...] = jnp.zeros_like(by_b)

    b0 = place[0] + place[5] * B_DEV + step * b_step
    for p in range(b_step // 2):
        halves = []
        for q in range(2):
            b = 2 * p + q
            b_label = count_at_or_above(b0 + b, v_off)
            x = jnp.where(base == b_label, v_ref[b].astype(jnp.float32), 0.0).astype(jnp.bfloat16)
            halves.append(lax.dot_general(pick, x, (((1,), (1,)), ((), ())), preferred_element_type=jnp.float32))
        for r in range(ranks):
            pair = jnp.concatenate([h[r * A_ROW:(r + 1) * A_ROW] for h in halves], axis=0)
            start = pl.multiple_of(step * (b_step * A_ROW) + 16 * p, 16)
            by_b[r, pl.ds(start, 16), pl.ds(0, D_DEV)] = pair.astype(jnp.bfloat16)

    @pl.when(step == pl.num_programs(0) - 1)
    def _():
        to = lax.broadcasted_iota(jnp.int32, (ROWS, ROWS), 0)
        source = lax.broadcasted_iota(jnp.int32, (ROWS, ROWS), 1)
        a = a_of(to)
        move = jnp.where(source == (to - a * B_DEV) * A_ROW + a, 1.0, 0.0).astype(jnp.bfloat16)
        for r in range(ranks):
            w_ref[r] = jnp.dot(move, by_b[r], preferred_element_type=jnp.float32).astype(jnp.bfloat16)


SMEM = pl.BlockSpec(memory_space=pltpu.SMEM)


def squeeze(ranks, table, v):
    b_step = 10
    return pl.pallas_call(
        functools.partial(squeeze_kernel, ranks),
        grid=(B_DEV // b_step,),
        in_specs=[SMEM, pl.BlockSpec((b_step, D_DEV, KB), lambda i: (i, 0, 0))],
        out_specs=pl.BlockSpec((ranks, ROWS, KB), lambda i: (0, 0, 0)),
        out_shape=jax.ShapeDtypeStruct((ranks, ROWS, KB), jnp.bfloat16),
        scratch_shapes=[pltpu.VMEM((ranks, ROWS, KB), jnp.bfloat16)],
        compiler_params=pltpu.CompilerParams(vmem_limit_bytes=40 * 2**20),
        cost_estimate=pl.CostEstimate(flops=2 * 5000 * 128 * 8 * ranks, bytes_accessed=2400000, transcendentals=0),
        name="squeeze",
    )(table, v)


def contract_kernel(table, w_ref, t0, t1, mine_ref, other_ref, tp, a_labels, bd_labels, tail, packed):
    place, a_off, v_off, c_off = parts_of(table)
    step = pl.program_id(0)

    @pl.when(step == 0)
    def _():
        tp[...] = jnp.zeros_like(tp)
        tail[...] = jnp.zeros_like(tail)
        packed[...] = jnp.zeros_like(packed)
        for j, t in enumerate((t0, t1)):
            for z in range(4):
                block = t[z].astype(jnp.float32)
                for h in range(2):
                    part = block[:, h * N_DEV:(h + 1) * N_DEV].astype(jnp.bfloat16)
                    tp[pl.ds((8 * j + 2 * z + h) * KB, D_DEV), :] = part
        row = lax.broadcasted_iota(jnp.int32, (ROWS, KB), 0)
        lane = lax.broadcasted_iota(jnp.int32, (ROWS, KB), 1)
        a = a_of(row)
        d_label = count_at_or_above(lane + place[1], v_off)
        for s in range(4):
            a_labels[s] = count_at_or_above(a + s * A_ROW, a_off)
        for s in range(2):
            bd_labels[s] = d_label ^ count_at_or_above(row - a * B_DEV + place[0] + s * 2 * B_DEV, v_off)

    base = (a_labels[step >> 1] ^ bd_labels[step & 1]).astype(jnp.float32).astype(jnp.bfloat16)
    acc = None
    for j in range(2):
        for z in range(0, 4, 2):
            masked = []
            for i in range(4):
                c = 4 * (z + i // 2) + 2 * (i % 2) + (place[3] ^ j)
                c_label = count_at_or_above(c, c_off)
                rank = jnp.minimum(c - c_off[c_label], w_ref.shape[2] - 1)
                w = w_ref[0, 0, rank]
                hit = base == c_label.astype(jnp.float32).astype(jnp.bfloat16)
                masked.append(jnp.where(hit, w, jnp.zeros_like(w)))
            rows = tp[pl.ds((8 * j + 2 * z) * KB, 4 * KB), :]
            term = jnp.dot(jnp.concatenate(masked, axis=1), rows, preferred_element_type=jnp.float32)
            acc = term if acc is None else acc + term
    tail[pl.ds(0, ROWS), pl.ds(0, LEFT)] = acc[:, TILES * KB:]
    for a in range(A_ROW):
        for t in range(TILES):
            packed[a, pl.ds(8 + t * B_DEV, B_DEV), :] = acc[a * B_DEV:(a + 1) * B_DEV, t * KB:(t + 1) * KB]
        left = tail[pl.ds(a * B_DEV, 8, stride=8), :]
        for s in range(1, 8):
            left = left + pltpu.roll(tail[pl.ds(a * B_DEV + s, 8, stride=8), :], LEFT * s, 1)
        packed[a, pl.ds(0, 8), :] = left
    for z in range(4):
        mine_ref[z] = packed[2 * z + place[4]].astype(jnp.bfloat16)
        other_ref[z] = packed[2 * z + 1 - place[4]].astype(jnp.bfloat16)


def contract(table, w, t0, t1):
    ranks = w.shape[2]
    t_spec = pl.BlockSpec((4, D_DEV, 2 * N_DEV), lambda i, tab: (0, 0, 0))
    o_spec = pl.BlockSpec((4, PACKED, KB), lambda i, tab: (i, 0, 0))
    o_shape = jax.ShapeDtypeStruct((4 * GROUPS, PACKED, KB), jnp.bfloat16)
    return pl.pallas_call(
        contract_kernel,
        grid_spec=pltpu.PrefetchScalarGridSpec(
            num_scalar_prefetch=1,
            grid=(GROUPS,),
            in_specs=[
                pl.BlockSpec((1, 1, ranks, ROWS, KB), lambda i, tab: (i >> 1, (i & 1) ^ tab[7], 0, 0, 0)),
                t_spec,
                t_spec,
            ],
            out_specs=[o_spec, o_spec],
            scratch_shapes=[
                pltpu.VMEM((CB * KB, N_DEV), jnp.bfloat16),
                pltpu.VMEM((4, ROWS, KB), jnp.int32),
                pltpu.VMEM((2, ROWS, KB), jnp.int32),
                pltpu.VMEM((ROWS + 16, KB), jnp.float32),
                pltpu.VMEM((A_ROW, PACKED, KB), jnp.float32),
            ],
        ),
        out_shape=[o_shape, o_shape],
        compiler_params=pltpu.CompilerParams(vmem_limit_bytes=50 * 2**20),
        cost_estimate=pl.CostEstimate(flops=2 * 3200 * 2048 * 400, bytes_accessed=10000000, transcendentals=0),
        name="contract",
    )(table, w, t0, t1)


def add_kernel(in_ref, out_ref, tail, rows):
    for g in range(GROUPS):
        total = in_ref[4 * g].astype(jnp.float32)
        for z in range(1, 4):
            total = total + in_ref[4 * g + z].astype(jnp.float32)
        for t in range(TILES):
            rows[:, pl.ds(g * N_DEV + t * KB, KB)] = total[8 + t * B_DEV:8 + (t + 1) * B_DEV]
        for s in range(8):
            part = total[0:8] if s == 0 else pltpu.roll(total[0:8], KB - LEFT * s, 1)
            tail[pl.ds(s, 8, stride=8), :] = part
        rows[:, pl.ds(g * N_DEV + TILES * KB, LEFT)] = tail[pl.ds(0, B_DEV), pl.ds(0, LEFT)]
    out_ref[0] = rows[...].astype(jnp.bfloat16)


def add_up(parts):
    vmem = pl.BlockSpec(memory_space=pltpu.VMEM)
    return pl.pallas_call(
        add_kernel,
        in_specs=[vmem],
        out_specs=vmem,
        out_shape=jax.ShapeDtypeStruct((1, B_DEV, GROUPS * N_DEV), jnp.bfloat16),
        scratch_shapes=[pltpu.VMEM((64, KB), jnp.float32), pltpu.VMEM((B_DEV, GROUPS * N_DEV), jnp.float32)],
        compiler_params=pltpu.CompilerParams(vmem_limit_bytes=20 * 2**20),
        name="add_up",
    )(parts)


def program(ranks, table, integrals, amplitudes):
    f32, bf16 = jnp.float32, jnp.bfloat16
    w = squeeze(ranks, table, integrals)
    beside = lax.ppermute(w, "yn", SWAP)
    t = lax.all_to_all(amplitudes.reshape(25, GROUPS, N_DEV).transpose(1, 0, 2), ("x", "yn"), 0, 0, tiled=True)
    t = t.reshape(4, 2, 25, N_DEV).transpose(0, 2, 1, 3).reshape(1, D_DEV, 2 * N_DEV)
    t, w, beside = lax.optimization_barrier((t, w, beside))
    w = lax.all_gather(jnp.stack([w, beside]), "x", axis=0)
    t = lax.all_gather(t, "zh", axis=0, tiled=True)
    mine, other = contract(table, w, t, lax.ppermute(t, "yt", SWAP))
    got = lax.ppermute(other, "core", SWAP)
    total = (mine.astype(f32) + got.astype(f32)).astype(bf16)
    return add_up(lax.all_to_all(total, ("x", "yn", "zl"), 0, 0, tiled=True))


def shards(integrals, amplitudes, a_offsets, vir_offsets, c_offsets):
    x, zh, zl, core = (lax.axis_index(name) for name in ("x", "zh", "zl", "core"))
    yn, yt = lax.axis_index("yn"), lax.axis_index("yt")
    place = [(zh * 4 + yt) * B_DEV, (zl * 2 + core) * D_DEV, x, yt, core, 2 * yn, zl, yn]
    table = jnp.concatenate([jnp.stack(place).astype(jnp.int32), a_offsets, vir_offsets, c_offsets])
    few, most = functools.partial(program, RANKS_FEW), functools.partial(program, RANKS_MOST)
    narrow = jnp.max(c_offsets[1:] - c_offsets[:-1]) <= RANKS_FEW
    return lax.cond(narrow, few, most, table, integrals, amplitudes)


def solution(mesh):
    fine = Mesh(mesh.devices.reshape(4, 4, 2, 2, 4, 2), ("x", "zh", "yn", "yt", "zl", "core"))
    b_and_c = ("zh", "yn", "yt")
    in_specs = (P(b_and_c, ("zl", "core"), "x"), P(b_and_c, ("zl", "core", "x"), None), P(), P(), P())
    out_specs = P(("x", "zl", "core"), b_and_c, None)
    return jax.shard_map(shards, mesh=fine, in_specs=in_specs, out_specs=out_specs, check_vma=False)
```

time: 360 us -> 157 us (0.44)
  waiting for transfers between devices: 314 us -> 16.2 us
  blocking collectives: 14.5 us -> 88.3 us
  Pallas kernels: 0 us -> 17.4 us
  starting transfers between devices: 0.08 us -> 14.4 us
  matrix products: 9.18 us -> 0 us
    all_gather x1, waiting for transfers between devices: 269 us -> 0.02 us  [program(): w = lax.all_gather(jnp.stack([w, beside]), 'x', axis=0)]
    all_to_all x0 -> x2, blocking collectives: none -> 51.9 us  [the longest x1 40.8 us: program(): return add_up(lax.all_to_all(total, ('x', 'yn', 'zl'), 0, 0, tiled=True))]
    unnamed x3 -> x0, waiting for transfers between devices: 45 us -> none
    all_gather x1, blocking collectives: 14.5 us -> 36.3 us  [program(): t = lax.all_gather(t, 'zh', axis=0, tiled=True)]
    pallas_call x0 -> x3, Pallas kernels: none -> 17.4 us  [the longest x1 12.2 us: contract(): pl.pallas_call(contract_kernel, grid_spec=pltpu.PrefetchScalarGridSpec(nu...]
    ppermute x0 -> x3, waiting for transfers between devices: none -> 16.2 us  [the longest x1 13.6 us: program(): mine, other = contract(table, w, t, lax.ppermute(t, 'yt', SWAP))]
    ppermute x0 -> x3, starting transfers between devices: none -> 14.3 us  [the longest x1 6.08 us: program(): got = lax.ppermute(other, 'core', SWAP)]
    dot_general x1 -> x0, matrix products: 9.18 us -> none  [shards(): jnp.einsum('bdac,cdk->abk', masked, lax.all_gather(local_amps, 'col', axi...]
  transfers between devices with their start and end apart: 2 -> 4, of which waited for: 2 -> 2; matrix products, arithmetic and copies ran while one was open for 1% -> 1% of each run, Pallas kernels for 0% -> 0%
where the time goes in v2:
time: 157 us; the launch traced here: 156 us
  blocking collectives  88.3 us (56%)
  Pallas kernels  17.4 us (11%)
  waiting for transfers between devices  16.2 us (10%)
  starting transfers between devices  14.4 us (9%)
  between operations  14.1 us (9%)
  local copies, waits for them, and re-layouts  2.79 us (2%)
  other arithmetic  2.75 us (2%)
    all_to_all x1, blocking collectives, program(): return add_up(lax.all_to_all(total, ('x', 'yn', 'zl'), 0, 0, tiled=True))  40.8 us
    all_gather x1, blocking collectives, program(): t = lax.all_gather(t, 'zh', axis=0, tiled=True)  36.3 us
    ppermute x1, waiting for transfers between devices, program(): mine, other = contract(table, w, t, lax.ppermute(t, 'yt', SWAP))  13.6 us
    pallas_call x1, Pallas kernels, contract(): pl.pallas_call(contract_kernel, grid_spec=pltpu.PrefetchScalarGridSpec(nu...  12.2 us
    all_to_all x1, blocking collectives, program(): lax.all_to_all(amplitudes.reshape(25, GROUPS, N_DEV).transpose(1, 0, 2),...  11.1 us
    ppermute x1, starting transfers between devices, program(): got = lax.ppermute(other, 'core', SWAP)  6.08 us
    ppermute x1, starting transfers between devices, program(): beside = lax.ppermute(w, 'yn', SWAP)  5.65 us
    pallas_call x1, Pallas kernels, squeeze(): pl.pallas_call(functools.partial(squeeze_kernel, ranks), grid=(B_DEV // b...  4.5 us
  transfers between devices with their start and end apart: 4, of which 2 were waited for; matrix products, arithmetic and copies ran while one was open for 1% of the time, Pallas kernels for 0%

profile of v2, /device:TPU:1, one launch (start us, length us, event | category | flops | bytes accessed | tf_op | source)
XLA Modules:
  0.0 156.2 jit_solution(17209776555504933566)
XLA Ops:
  6.5 1.4 subtract_reduce_fusion
  8.6 0.8 concatenate.3
  9.4 139.2 %conditional.1 = (bf16[1,50,3200]{2,1,0:T(8,128)(2,1)S(1)}) conditional(s32[]{:T(128)} %convert_element_type.21, (bf16[1,25,3200]{2,1,0:T(8,128)(2,1)}, s32[35]{0:T(128)S(1)}, bf16[50,100,128]{2,1,0:T(8,128)(2,1)}) %tuple.13, (bf16[1,25,3200]{2,1,0:T(8,128)(2,1)}, s32[35]{0:T(128)S(1)}, bf16[50,100,128]{2,1,0:T(8,128)(2,1)}) %tuple.13), branch_computations={%region_1.0_spmd, %region_2.0_spmd} | conditional | flops 5338583040 | bytes 67377480 | solution.py:248
  9.4 0.0 all-gather.7.cloned.1.call-start
  9.5 4.5 %squeeze.3 = bf16[3,400,128]{2,1,0:T(8,128)(2,1)S(1)} custom-call(s32[35]{0:T(128)S(1)} %get-tuple-element.28.table, bf16[50,100,128]{2,1,0:T(8,128)(2,1)} %get-tuple-element.44.v_ref), custom_call_target="tpu_custom_call" | custom-call | flops 30720000 | bytes 2400000 | tf_op jit(solution)/shard_map/cond/branch_1_fun/squeeze/pallas_call | solution.py:103
  14.0 5.7 %collective-permute-start.3 = (bf16[3,400,128]{2,1,0:T(8,128)(2,1)S(1)}, bf16[3,400,128]{2,1,0:T(8,128)(2,1)S(1)}, u32[]{:S(2)}, u32[]{:S(2)}) collective-permute-start(bf16[3,400,128]{2,1,0:T(8,128)(2,1)S(1)} %squeeze.3), channel_id=1, source_target_pairs={{0,16},{16,0},{1,17},{17,1},{2,18},{18,2},{3,19},{19,3},{4,20},{20... | collective-permute-start | bytes 921608 | tf_op jit(solution)/shard_map/cond/branch_1_fun/ppermute | solution.py:229
  19.6 0.5 reshape.15
  20.1 0.1 copy.25
  20.2 11.1 %all_to_all.18 = bf16[8,25,400]{2,1,0:T(8,128)(2,1)S(1)} all-to-all(bf16[8,25,400]{2,1,0:T(8,128)(2,1)S(1)} %copy.25), channel_id=1, replica_groups=mesh['x'=4,'zh'=4,'yn'=2,'yt'=2,'zl'=4,'core'=2] {'x','yn'}, dimensions={0} | all-to-all | bytes 320000 | tf_op jit(solution)/shard_map/cond/branch_1_fun/all_to_all | solution.py:230
  31.3 0.2 copy.37
  31.5 0.2 reshape.17
  31.7 0.9 pad_maximum_fusion.1
  32.6 36.3 %all_gather.17.t0 = bf16[4,100,800]{2,1,0:T(8,128)(2,1)S(1)} all-gather(bf16[1,100,800]{2,1,0:T(8,128)(2,1)S(1)} %reshape.17), channel_id=1, replica_groups=mesh['x'=4,'zh'=4,'yn'=2,'yt'=2,'zl'=4,'core'=2] {'zh'}, dimensions={0}, use_global_device_ids=true | all-gather | bytes 800000 | tf_op jit(solution)/shard_map/cond/branch_1_fun/all_gather | solution.py:234
  69.0 0.3 copy.28
  69.2 2.6 %collective-permute-start.4 = (bf16[4,100,800]{2,0,1:T(4,128)(2,1)S(1)}, bf16[4,100,800]{2,0,1:T(4,128)(2,1)S(1)}, u32[]{:S(2)}, u32[]{:S(2)}) collective-permute-start(bf16[4,100,800]{2,0,1:T(4,128)(2,1)S(1)} %copy.28), channel_id=1, source_target_pairs={{0,8},{8,0},{1,9},{9,1},{2,10},{10,2},{3,11},{11,3},{4,12},{12,4},... | collective-permute-start | bytes 1920008 | tf_op jit(solution)/shard_map/cond/branch_1_fun/ppermute | solution.py:235
  71.9 13.6 %collective-permute-done.4 = bf16[4,100,800]{2,0,1:T(4,128)(2,1)S(1)} collective-permute-done((bf16[4,100,800]{2,0,1:T(4,128)(2,1)S(1)}, bf16[4,100,800]{2,0,1:T(4,128)(2,1)S(1)}, u32[]{:S(2)}, u32[]{:S(2)}) %collective-permute-start.4) | collective-permute-done | bytes 640032 | tf_op jit(solution)/shard_map/cond/branch_1_fun/ppermute | solution.py:235
  85.4 0.1 copy.29.t1
  85.5 12.2 %contract.3 = (bf16[32,160,128]{2,1,0:T(8,128)(2,1)S(1)}, bf16[32,160,128]{2,1,0:T(8,128)(2,1)S(1)}) custom-call(s32[35]{0:T(128)S(1)} %get-tuple-element.28.table, bf16[4,2,3,400,128]{4,3,2,1,0:T(8,128)(2,1)} %bitcast.37, bf16[4,100,800]{2,1,0:T(8,128)(2,1)S(1)} %all_gather.17.t0, bf16[4,100,800]{2,1,0:T(8,128)(2,1)S(1)} %copy.29.t1), custom_call_target="tpu_custom_call" | custom-call | flops 5242880000 | bytes 10000000 | tf_op jit(solution)/shard_map/cond/branch_1_fun/contract/pallas_call | solution.py:173
  97.7 6.1 %collective-permute-start.5 = (bf16[32,160,128]{2,1,0:T(8,128)(2,1)S(1)}, bf16[32,160,128]{2,1,0:T(8,128)(2,1)S(1)}, u32[]{:S(2)}, u32[]{:S(2)}) collective-permute-start(bf16[32,160,128]{2,1,0:T(8,128)(2,1)S(1)} %get-tuple-element.35), channel_id=1, source_target_pairs={{0,1},{1,0},{2,3},{3,2},{4,5},{5,4},{6,7},{7,6},{8,9},{9,8},{10,11... | collective-permute-start | bytes 3932168 | tf_op jit(solution)/shard_map/cond/branch_1_fun/ppermute | solution.py:236
  103.8 2.6 %collective-permute-done.5 = bf16[32,160,128]{2,1,0:T(8,128)(2,1)S(1)} collective-permute-done((bf16[32,160,128]{2,1,0:T(8,128)(2,1)S(1)}, bf16[32,160,128]{2,1,0:T(8,128)(2,1)S(1)}, u32[]{:S(2)}, u32[]{:S(2)}) %collective-permute-start.5) | collective-permute-done | bytes 1310752 | tf_op jit(solution)/shard_map/cond/branch_1_fun/ppermute | solution.py:236
  106.5 0.4 add_convert_fusion.1
  106.9 40.8 %all_to_all.19.in_ref = bf16[32,160,128]{2,1,0:T(8,128)(2,1)S(1)} all-to-all(bf16[32,160,128]{2,1,0:T(8,128)(2,1)S(1)} %add_convert_fusion.1), channel_id=1, replica_groups=mesh['x'=4,'zh'=4,'yn'=2,'yt'=2,'zl'=4,'core'=2] {'x','yn','zl'}, dimensions={0} | all-to-all | bytes 2621440 | tf_op jit(solution)/shard_map/cond/branch_1_fun/all_to_all | solution.py:238
  147.7 0.7 add_up.3
  148.6 0.7 copy-done.2
  (6 shorter events, 0.0 us)
Async XLA Ops:
  9.4 10.2 %copy-start.1 = (bf16[1,25,3200]{2,1,0:T(8,128)(2,1)S(1)}, bf16[1,25,3200]{2,1,0:T(8,128)(2,1)}, u32[]{:S(2)}) copy-start(bf16[1,25,3200]{2,1,0:T(8,128)(2,1)} %get-tuple-element.42) | copy-start | bytes 480004 | tf_op jit(solution)/shard_map/cond
  9.4 76.1 %all-gather.7.cloned.1.call-start = ((), (), s32[]{:S(2)}) async-start(), calls=%async_computation.5 | async-start | bytes 3072000 | tf_op jit(solution)/shard_map/cond/branch_1_fun/all_gather | solution.py:233
  14.0 17.7 %collective-permute-start.3 = (bf16[3,400,128]{2,1,0:T(8,128)(2,1)S(1)}, bf16[3,400,128]{2,1,0:T(8,128)(2,1)S(1)}, u32[]{:S(2)}, u32[]{:S(2)}) collective-permute-start(bf16[3,400,128]{2,1,0:T(8,128)(2,1)S(1)} %squeeze.3), channel_id=1, source_target_pairs={{0,16},{16,0},{1,17},{17,1},{2,18},{18,2},{3,19},{19,3},{4,20},{20... | collective-permute-start | bytes 921608 | tf_op jit(solution)/shard_map/cond/branch_1_fun/ppermute | solution.py:229
  69.2 16.2 %collective-permute-start.4 = (bf16[4,100,800]{2,0,1:T(4,128)(2,1)S(1)}, bf16[4,100,800]{2,0,1:T(4,128)(2,1)S(1)}, u32[]{:S(2)}, u32[]{:S(2)}) collective-permute-start(bf16[4,100,800]{2,0,1:T(4,128)(2,1)S(1)} %copy.28), channel_id=1, source_target_pairs={{0,8},{8,0},{1,9},{9,1},{2,10},{10,2},{3,11},{11,3},{4,12},{12,4},... | collective-permute-start | bytes 1920008 | tf_op jit(solution)/shard_map/cond/branch_1_fun/ppermute | solution.py:235
  97.7 8.7 %collective-permute-start.5 = (bf16[32,160,128]{2,1,0:T(8,128)(2,1)S(1)}, bf16[32,160,128]{2,1,0:T(8,128)(2,1)S(1)}, u32[]{:S(2)}, u32[]{:S(2)}) collective-permute-start(bf16[32,160,128]{2,1,0:T(8,128)(2,1)S(1)} %get-tuple-element.35), channel_id=1, source_target_pairs={{0,1},{1,0},{2,3},{3,2},{4,5},{5,4},{6,7},{7,6},{8,9},{9,8},{10,11... | collective-permute-start | bytes 3932168 | tf_op jit(solution)/shard_map/cond/branch_1_fun/ppermute | solution.py:236
  148.6 0.7 copy-start.2
Sparse Core Ops, SparseCore 0:
  32.7 44.6 all-gather.6

commit v3 on v2

--- a/solution.py
+++ b/solution.py
@@ -113,87 +113,143 @@
     )(table, v)
 
 
-def contract_kernel(table, w_ref, t0, t1, mine_ref, other_ref, tp, a_labels, bd_labels, tail, packed):
-    place, a_off, v_off, c_off = parts_of(table)
+def fill_rows(tp, t):
+    tp[...] = jnp.zeros_like(tp)
+    for z in range(4):
+        block = t[z].astype(jnp.float32)
+        for h in range(2):
+            part = block[:, h * N_DEV:(h + 1) * N_DEV].astype(jnp.bfloat16)
+            tp[pl.ds((2 * z + h) * KB, D_DEV), :] = part
+
+
+def fill_labels(table, a_labels, bd_labels):
+    place, a_off, v_off, _ = parts_of(table)
+    row = lax.broadcasted_iota(jnp.int32, (ROWS, KB), 0)
+    lane = lax.broadcasted_iota(jnp.int32, (ROWS, KB), 1)
+    a = a_of(row)
+    d_label = count_at_or_above(lane + place[1], v_off)
+    for s in range(4):
+        a_labels[s] = count_at_or_above(a + s * A_ROW, a_off)
+    for s in range(2):
+        bd_labels[s] = d_label ^ count_at_or_above(row - a * B_DEV + place[0] + s * 2 * B_DEV, v_off)
+
+
+def x_at(step, table):
+    return (table[2] + (step >> 1)) & 3
+
+
+def yn_at(step, table):
+    return table[7] ^ (step & 1)
+
+
+def product(table, step, w_ref, yt, tp, a_labels, bd_labels):
+    c_off = parts_of(table)[3]
+    base = (a_labels[x_at(step, table)] ^ bd_labels[yn_at(step, table)]).astype(jnp.float32).astype(jnp.bfloat16)
+    masked = []
+    for z in range(4):
+        for h in range(2):
+            c = 4 * z + 2 * h + yt
+            c_label = count_at_or_above(c, c_off)
+            rank = jnp.minimum(c - c_off[c_label], w_ref.shape[1] - 1)
+            w = w_ref[step & 1, rank]
+            hit = base == c_label.astype(jnp.float32).astype(jnp.bfloat16)
+            masked.append(jnp.where(hit, w, jnp.zeros_like(w)))
+    return jnp.dot(jnp.concatenate(masked, axis=1), tp[...], preferred_element_type=jnp.float32)
+
+
+def early_kernel(table, w0, w1, w2, w3, t, out_ref, tp, a_labels, bd_labels):
     step = pl.program_id(0)
 
     @pl.when(step == 0)
     def _():
-        tp[...] = jnp.zeros_like(tp)
+        fill_rows(tp, t)
+        fill_labels(table, a_labels, bd_labels)
+
+    for j, w in enumerate((w0, w1, w2, w3)):
+        @pl.when(step >> 1 == j)
+        def _(w=w):
+            out_ref[0] = product(table, step, w, table[3], tp, a_labels, bd_labels)
+
+
+def late_kernel(table, w0, w1, w2, w3, t, part_ref, mine_ref, other_ref, tp, a_labels, bd_labels, acc, tail, packed):
+    step = pl.program_id(0)
+
+    @pl.when(step == 0)
+    def _():
+        fill_rows(tp, t)
+        fill_labels(table, a_labels, bd_labels)
         tail[...] = jnp.zeros_like(tail)
         packed[...] = jnp.zeros_like(packed)
-        for j, t in enumerate((t0, t1)):
-            for z in range(4):
-                block = t[z].astype(jnp.float32)
-                for h in range(2):
-                    part = block[:, h * N_DEV:(h + 1) * N_DEV].astype(jnp.bfloat16)
-                    tp[pl.ds((8 * j + 2 * z + h) * KB, D_DEV), :] = part
-        row = lax.broadcasted_iota(jnp.int32, (ROWS, KB), 0)
-        lane = lax.broadcasted_iota(jnp.int32, (ROWS, KB), 1)
-        a = a_of(row)
-        d_label = count_at_or_above(lane + place[1], v_off)
-        for s in range(4):
-            a_labels[s] = count_at_or_above(a + s * A_ROW, a_off)
-        for s in range(2):
-            bd_labels[s] = d_label ^ count_at_or_above(row - a * B_DEV + place[0] + s * 2 * B_DEV, v_off)
-
-    base = (a_labels[step >> 1] ^ bd_labels[step & 1]).astype(jnp.float32).astype(jnp.bfloat16)
-    acc = None
-    for j in range(2):
-        for z in range(0, 4, 2):
-            masked = []
-            for i in range(4):
-                c = 4 * (z + i // 2) + 2 * (i % 2) + (place[3] ^ j)
-                c_label = count_at_or_above(c, c_off)
-                rank = jnp.minimum(c - c_off[c_label], w_ref.shape[2] - 1)
-                w = w_ref[0, 0, rank]
-                hit = base == c_label.astype(jnp.float32).astype(jnp.bfloat16)
-                masked.append(jnp.where(hit, w, jnp.zeros_like(w)))
-            rows = tp[pl.ds((8 * j + 2 * z) * KB, 4 * KB), :]
-            term = jnp.dot(jnp.concatenate(masked, axis=1), rows, preferred_element_type=jnp.float32)
-            acc = term if acc is None else acc + term
+
+    for j, w in enumerate((w0, w1, w2, w3)):
+        @pl.when(step >> 1 == j)
+        def _(w=w):
+            acc[...] = part_ref[0] + product(table, step, w, 1 - table[3], tp, a_labels, bd_labels)
+
     tail[pl.ds(0, ROWS), pl.ds(0, LEFT)] = acc[:, TILES * KB:]
     for a in range(A_ROW):
-        for t in range(TILES):
-            packed[a, pl.ds(8 + t * B_DEV, B_DEV), :] = acc[a * B_DEV:(a + 1) * B_DEV, t * KB:(t + 1) * KB]
+        for s in range(TILES):
+            packed[a, pl.ds(8 + s * B_DEV, B_DEV), :] = acc[a * B_DEV:(a + 1) * B_DEV, s * KB:(s + 1) * KB]
         left = tail[pl.ds(a * B_DEV, 8, stride=8), :]
         for s in range(1, 8):
             left = left + pltpu.roll(tail[pl.ds(a * B_DEV + s, 8, stride=8), :], LEFT * s, 1)
         packed[a, pl.ds(0, 8), :] = left
     for z in range(4):
-        mine_ref[z] = packed[2 * z + place[4]].astype(jnp.bfloat16)
-        other_ref[z] = packed[2 * z + 1 - place[4]].astype(jnp.bfloat16)
-
-
-def contract(table, w, t0, t1):
-    ranks = w.shape[2]
-    t_spec = pl.BlockSpec((4, D_DEV, 2 * N_DEV), lambda i, tab: (0, 0, 0))
-    o_spec = pl.BlockSpec((4, PACKED, KB), lambda i, tab: (i, 0, 0))
-    o_shape = jax.ShapeDtypeStruct((4 * GROUPS, PACKED, KB), jnp.bfloat16)
+        mine_ref[z] = packed[2 * z + table[4]].astype(jnp.bfloat16)
+        other_ref[z] = packed[2 * z + 1 - table[4]].astype(jnp.bfloat16)
+
+
+SCRATCH = [
+    pltpu.VMEM((CB // 2 * KB, N_DEV), jnp.bfloat16),
+    pltpu.VMEM((4, ROWS, KB), jnp.int32),
+    pltpu.VMEM((2, ROWS, KB), jnp.int32),
+]
+PART = pl.BlockSpec((1, ROWS, N_DEV), lambda i, tab: (i, 0, 0))
+
+
+def operands(ranks):
+    w_spec = pl.BlockSpec((2, ranks, ROWS, KB), lambda i, tab: (0, 0, 0, 0))
+    return [w_spec] * 4 + [pl.BlockSpec((4, D_DEV, 2 * N_DEV), lambda i, tab: (0, 0, 0))]
+
+
+def early(table, ws, t):
     return pl.pallas_call(
-        contract_kernel,
+        early_kernel,
         grid_spec=pltpu.PrefetchScalarGridSpec(
             num_scalar_prefetch=1,
             grid=(GROUPS,),
-            in_specs=[
-                pl.BlockSpec((1, 1, ranks, ROWS, KB), lambda i, tab: (i >> 1, (i & 1) ^ tab[7], 0, 0, 0)),
-                t_spec,
-                t_spec,
-            ],
+            in_specs=operands(ws[0].shape[1]),
+            out_specs=PART,
+            scratch_shapes=SCRATCH,
+        ),
+        out_shape=jax.ShapeDtypeStruct((GROUPS, ROWS, N_DEV), jnp.float32),
+        compiler_params=pltpu.CompilerParams(vmem_limit_bytes=50 * 2**20),
+        cost_estimate=pl.CostEstimate(flops=2 * 3200 * 1024 * 400, bytes_accessed=9000000, transcendentals=0),
+        name="early",
+    )(table, *ws, t)
+
+
+def late(table, ws, t, partial):
+    o_spec = pl.BlockSpec((4, PACKED, KB), lambda i, tab: (2 * x_at(i, tab) + yn_at(i, tab), 0, 0))
+    o_shape = jax.ShapeDtypeStruct((4 * GROUPS, PACKED, KB), jnp.bfloat16)
+    return pl.pallas_call(
+        late_kernel,
+        grid_spec=pltpu.PrefetchScalarGridSpec(
+            num_scalar_prefetch=1,
+            grid=(GROUPS,),
+            in_specs=operands(ws[0].shape[1]) + [PART],
             out_specs=[o_spec, o_spec],
-            scratch_shapes=[
-                pltpu.VMEM((CB * KB, N_DEV), jnp.bfloat16),
-                pltpu.VMEM((4, ROWS, KB), jnp.int32),
-                pltpu.VMEM((2, ROWS, KB), jnp.int32),
+            scratch_shapes=SCRATCH + [
+                pltpu.VMEM((ROWS, N_DEV), jnp.float32),
                 pltpu.VMEM((ROWS + 16, KB), jnp.float32),
                 pltpu.VMEM((A_ROW, PACKED, KB), jnp.float32),
             ],
         ),
         out_shape=[o_shape, o_shape],
         compiler_params=pltpu.CompilerParams(vmem_limit_bytes=50 * 2**20),
-        cost_estimate=pl.CostEstimate(flops=2 * 3200 * 2048 * 400, bytes_accessed=10000000, transcendentals=0),
-        name="contract",
-    )(table, w, t0, t1)
+        cost_estimate=pl.CostEstimate(flops=2 * 3200 * 1024 * 400, bytes_accessed=11000000, transcendentals=0),
+        name="late",
+    )(table, *ws, t, partial)
 
 
 def add_kernel(in_ref, out_ref, tail, rows):
@@ -223,29 +279,44 @@
     )(parts)
 
 
-def program(ranks, table, integrals, amplitudes):
+def turn(k):
+    return [(i, (i - k) % 4) for i in range(4)]
+
+
+def around(w):
+    return [w] + [lax.ppermute(w, "x", turn(k)) for k in (1, 2, 3)]
+
+
+def again(table, integrals, ws, own, beside, partial):
+    w = squeeze(RANKS_MOST, table, integrals)
+    ws = around(jnp.stack([w, lax.ppermute(w, "yn", SWAP)]))
+    return late(table, ws, beside, early(table, ws, own))
+
+
+def finish(table, integrals, ws, own, beside, partial):
+    return late(table, ws, beside, partial)
+
+
+def shards(integrals, amplitudes, a_offsets, vir_offsets, c_offsets):
     f32, bf16 = jnp.float32, jnp.bfloat16
-    w = squeeze(ranks, table, integrals)
-    beside = lax.ppermute(w, "yn", SWAP)
-    t = lax.all_to_all(amplitudes.reshape(25, GROUPS, N_DEV).transpose(1, 0, 2), ("x", "yn"), 0, 0, tiled=True)
-    t = t.reshape(4, 2, 25, N_DEV).transpose(0, 2, 1, 3).reshape(1, D_DEV, 2 * N_DEV)
-    t, w, beside = lax.optimization_barrier((t, w, beside))
-    w = lax.all_gather(jnp.stack([w, beside]), "x", axis=0)
-    t = lax.all_gather(t, "zh", axis=0, tiled=True)
-    mine, other = contract(table, w, t, lax.ppermute(t, "yt", SWAP))
-    got = lax.ppermute(other, "core", SWAP)
-    total = (mine.astype(f32) + got.astype(f32)).astype(bf16)
-    return add_up(lax.all_to_all(total, ("x", "yn", "zl"), 0, 0, tiled=True))
-
-
-def shards(integrals, amplitudes, a_offsets, vir_offsets, c_offsets):
     x, zh, zl, core = (lax.axis_index(name) for name in ("x", "zh", "zl", "core"))
     yn, yt = lax.axis_index("yn"), lax.axis_index("yt")
     place = [(zh * 4 + yt) * B_DEV, (zl * 2 + core) * D_DEV, x, yt, core, 2 * yn, zl, yn]
     table = jnp.concatenate([jnp.stack(place).astype(jnp.int32), a_offsets, vir_offsets, c_offsets])
-    few, most = functools.partial(program, RANKS_FEW), functools.partial(program, RANKS_MOST)
     narrow = jnp.max(c_offsets[1:] - c_offsets[:-1]) <= RANKS_FEW
-    return lax.cond(narrow, few, most, table, integrals, amplitudes)
+    w = squeeze(RANKS_FEW, table, integrals)
+    w_beside = lax.ppermute(w, "yn", SWAP)
+    t = lax.all_to_all(amplitudes.reshape(25, GROUPS, N_DEV).transpose(1, 0, 2), ("x", "yn"), 0, 0, tiled=True)
+    t = t.reshape(4, 2, 25, N_DEV).transpose(0, 2, 1, 3).reshape(1, D_DEV, 2 * N_DEV)
+    t, w, w_beside = lax.optimization_barrier((t, w, w_beside))
+    ws = around(jnp.stack([w, w_beside]))
+    own = lax.all_gather(t, "zh", axis=0, tiled=True)
+    beside = lax.ppermute(own, "yt", SWAP)
+    partial = early(table, ws, own)
+    mine, other = lax.cond(narrow, finish, again, table, integrals, ws, own, beside, partial)
+    got = lax.ppermute(other, "core", SWAP)
+    total = (mine.astype(f32) + got.astype(f32)).astype(bf16)
+    return add_up(lax.all_to_all(total, ("x", "yn", "zl"), 0, 0, tiled=True))
 
 
 def solution(mesh):

time: 157 us -> 147 us (0.936)
  between operations: 14.1 us -> 0.83 us
  starting transfers between devices: 14.4 us -> 25.9 us
  waiting for transfers between devices: 16.2 us -> 4.88 us
  Pallas kernels: 17.4 us -> 22.6 us
  other arithmetic: 2.75 us -> 1.1 us
    ppermute x3 -> x6, starting transfers between devices: 14.3 us -> 25.9 us  [the longest x3 8.97 us: around(): return [w] + [lax.ppermute(w, 'x', turn(k)) for k in (1, 2, 3)]]
    ppermute x3 -> x6, waiting for transfers between devices: 16.2 us -> 4.88 us  [the longest x1 2.64 us: shards(): got = lax.ppermute(other, 'core', SWAP)]
    pallas_call x1 -> x2, Pallas kernels: 12.2 us -> 16.7 us  [the longest x1 9.1 us: late(): pl.pallas_call(late_kernel, grid_spec=pltpu.PrefetchScalarGridSpec(num_sc...]
    all_to_all x2, blocking collectives: 51.9 us -> 49.8 us  [the longest x1 38.7 us: shards(): return add_up(lax.all_to_all(total, ('x', 'yn', 'zl'), 0, 0, tiled=True))]
    all_gather x1, blocking collectives: 36.3 us -> 38.3 us  [shards(): own = lax.all_gather(t, 'zh', axis=0, tiled=True)]
  transfers between devices with their start and end apart: 4 -> 6, of which waited for: 2 -> 2; matrix products, arithmetic and copies ran while one was open for 1% -> 2% of each run, Pallas kernels for 0% -> 5%
where the time goes in v3:
time: 147 us; the launch traced here: 146 us
  blocking collectives  88.1 us (60%)
  starting transfers between devices  25.9 us (18%)
  Pallas kernels  22.6 us (15%)
  waiting for transfers between devices  4.88 us (3%)
  local copies, waits for them, and re-layouts  2.99 us (2%)
    all_to_all x1, blocking collectives, shards(): return add_up(lax.all_to_all(total, ('x', 'yn', 'zl'), 0, 0, tiled=True))  38.7 us
    all_gather x1, blocking collectives, shards(): own = lax.all_gather(t, 'zh', axis=0, tiled=True)  38.3 us
    all_to_all x1, blocking collectives, shards(): lax.all_to_all(amplitudes.reshape(25, GROUPS, N_DEV).transpose(1, 0, 2),...  11.1 us
    pallas_call x1, Pallas kernels, late(): pl.pallas_call(late_kernel, grid_spec=pltpu.PrefetchScalarGridSpec(num_sc...  9.1 us
    ppermute x3, starting transfers between devices, around(): return [w] + [lax.ppermute(w, 'x', turn(k)) for k in (1, 2, 3)]  8.97 us
    ppermute x1, starting transfers between devices, shards(): got = lax.ppermute(other, 'core', SWAP)  7.85 us
    pallas_call x1, Pallas kernels, early(): pl.pallas_call(early_kernel, grid_spec=pltpu.PrefetchScalarGridSpec(num_s...  7.6 us
    ppermute x1, starting transfers between devices, shards(): w_beside = lax.ppermute(w, 'yn', SWAP)  5.65 us
  transfers between devices with their start and end apart: 6, of which 2 were waited for; matrix products, arithmetic and copies ran while one was open for 2% of the time, Pallas kernels for 5%

profile of v3, /device:TPU:1, one launch (start us, length us, event | category | flops | bytes accessed | tf_op | source)
XLA Modules:
  0.0 146.4 jit_solution(14090540061437351171)
XLA Ops:
  0.0 0.8 concatenate.3.table
  0.8 4.5 %squeeze.3 = bf16[3,400,128]{2,1,0:T(8,128)(2,1)S(1)} custom-call(s32[35]{0:T(128)S(1)} %concatenate.3.table, bf16[50,100,128]{2,1,0:T(8,128)(2,1)} %v_ref.1), custom_call_target="tpu_custom_call" | custom-call | flops 30720000 | bytes 2400000 | tf_op jit(solution)/shard_map/squeeze/pallas_call | solution.py:103
  5.3 5.7 %collective-permute-start.4 = (bf16[3,400,128]{2,1,0:T(8,128)(2,1)S(1)}, bf16[3,400,128]{2,1,0:T(8,128)(2,1)S(1)}, u32[]{:S(2)}, u32[]{:S(2)}) collective-permute-start(bf16[3,400,128]{2,1,0:T(8,128)(2,1)S(1)} %squeeze.3), channel_id=1, source_target_pairs={{0,16},{16,0},{1,17},{17,1},{2,18},{18,2},{3,19},{19,3},{4,20},{20... | collective-permute-start | bytes 921608 | tf_op jit(solution)/shard_map/ppermute | solution.py:308
  10.9 0.5 reshape.9
  11.5 11.1 %all_to_all.10 = bf16[8,25,400]{2,1,0:T(8,128)(2,1)S(1)} all-to-all(bf16[8,25,400]{2,1,0:T(8,128)(2,1)S(1)} %copy.11), channel_id=1, replica_groups=mesh['x'=4,'zh'=4,'yn'=2,'yt'=2,'zl'=4,'core'=2] {'x','yn'}, dimensions={0} | all-to-all | bytes 320000 | tf_op jit(solution)/shard_map/all_to_all | solution.py:309
  22.6 0.2 copy.20
  22.8 0.2 reshape.11
  23.1 1.9 %collective-permute-start.8 = (bf16[2,3,400,128]{3,2,1,0:T(8,128)(2,1)S(1)}, bf16[2,3,400,128]{3,2,1,0:T(8,128)(2,1)S(1)}, u32[]{:S(2)}, u32[]{:S(2)}) collective-permute-start(bf16[2,3,400,128]{3,2,1,0:T(8,128)(2,1)S(1)} %pad_maximum_fusion.1.w0), channel_id=1, source_target_pairs={{0,128},{128,256},{256,384},{384,0},{1,129},{129,257},{257,385},{3... | collective-permute-start | bytes 1843208 | tf_op jit(solution)/shard_map/ppermute | solution.py:287
  25.0 3.9 %collective-permute-start.7 = (bf16[2,3,400,128]{3,2,1,0:T(8,128)(2,1)S(1)}, bf16[2,3,400,128]{3,2,1,0:T(8,128)(2,1)S(1)}, u32[]{:S(2)}, u32[]{:S(2)}) collective-permute-start(bf16[2,3,400,128]{3,2,1,0:T(8,128)(2,1)S(1)} %pad_maximum_fusion.1.w0), channel_id=1, source_target_pairs={{0,256},{128,384},{256,0},{384,128},{1,257},{129,385},{257,1},{385... | collective-permute-start | bytes 1843208 | tf_op jit(solution)/shard_map/ppermute | solution.py:287
  28.9 3.2 %collective-permute-start.6 = (bf16[2,3,400,128]{3,2,1,0:T(8,128)(2,1)S(1)}, bf16[2,3,400,128]{3,2,1,0:T(8,128)(2,1)}, u32[]{:S(2)}, u32[]{:S(2)}) collective-permute-start(bf16[2,3,400,128]{3,2,1,0:T(8,128)(2,1)S(1)} %pad_maximum_fusion.1.w0), channel_id=1, source_target_pairs={{0,384},{128,0},{256,128},{384,256},{1,385},{129,1},{257,129},{385... | collective-permute-start | bytes 1843208 | tf_op jit(solution)/shard_map/ppermute | solution.py:287
  32.1 38.3 %all_gather.3.t = bf16[4,100,800]{2,1,0:T(8,128)(2,1)S(1)} all-gather(bf16[1,100,800]{2,1,0:T(8,128)(2,1)S(1)} %reshape.11), channel_id=1, replica_groups=mesh['x'=4,'zh'=4,'yn'=2,'yt'=2,'zl'=4,'core'=2] {'zh'}, dimensions={0}, use_global_device_ids=true | all-gather | bytes 800000 | tf_op jit(solution)/shard_map/all_gather | solution.py:313
  70.4 1.2 copy.14
  71.6 3.5 %collective-permute-start.5 = (bf16[4,100,800]{2,0,1:T(4,128)(2,1)}, bf16[4,100,800]{2,0,1:T(4,128)(2,1)S(1)}, u32[]{:S(2)}, u32[]{:S(2)}) collective-permute-start(bf16[4,100,800]{2,0,1:T(4,128)(2,1)} %copy.14), channel_id=1, source_target_pairs={{0,8},{8,0},{1,9},{9,1},{2,10},{10,2},{3,11},{11,3},{4,12},{12,4},... | collective-permute-start | bytes 1920008 | tf_op jit(solution)/shard_map/ppermute | solution.py:314
  75.0 0.7 subtract_reduce_fusion
  76.4 7.6 %early.3 = f32[8,400,400]{2,1,0:T(8,128)S(1)} custom-call(s32[35]{0:T(128)S(1)} %concatenate.3.table, bf16[2,3,400,128]{3,2,1,0:T(8,128)(2,1)S(1)} %pad_maximum_fusion.1.w0, bf16[2,3,400,128]{3,2,1,0:T(8,128)(2,1)} %collective-permute-done.6.w1, bf16[2,3,400,128]{3,2,1,0:T(8,128)(2,1)S(1)} %collective-permute-done.7.w2, ...), custom_call_target="tpu_custom_call" | custom-call | flops 2621440000 | bytes 9000000 | tf_op jit(solution)/shard_map/early/pallas_call | solution.py:216
  84.0 2.2 %collective-permute-done.5 = bf16[4,100,800]{2,0,1:T(4,128)(2,1)S(1)} collective-permute-done((bf16[4,100,800]{2,0,1:T(4,128)(2,1)}, bf16[4,100,800]{2,0,1:T(4,128)(2,1)S(1)}, u32[]{:S(2)}, u32[]{:S(2)}) %collective-permute-start.5) | collective-permute-done | bytes 640032 | tf_op jit(solution)/shard_map/ppermute | solution.py:314
  86.3 9.2 %conditional.2 = (bf16[32,160,128]{2,1,0:T(8,128)(2,1)S(1)}, bf16[32,160,128]{2,1,0:T(8,128)(2,1)S(1)}) conditional(s32[]{:T(128)} %convert_element_type.15, (s32[35]{0:T(128)S(1)}, bf16[50,100,128]{2,1,0:T(8,128)(2,1)S(1)}, bf16[4,100,800]{2,1,0:T(8,128)(2,1)S(1)}, bf16[4,100,800]{2,0,1:T(4,128)(2,1)S(1)}) %tuple.28, (s32[35]{0:T(128)S(1)}, ...), branch_computations={%region_1.0_spmd, %region_2.0_spmd} | conditional | flops 5335961600 | bytes 75289856
  86.3 0.1 copy.16.t
  86.4 9.1 %late.3 = (bf16[32,160,128]{2,1,0:T(8,128)(2,1)S(1)}, bf16[32,160,128]{2,1,0:T(8,128)(2,1)S(1)}) custom-call(s32[35]{0:T(128)S(1)} %get-tuple-element.41.table, bf16[2,3,400,128]{3,2,1,0:T(8,128)(2,1)S(1)} %get-tuple-element.42.w0, bf16[2,3,400,128]{3,2,1,0:T(8,128)(2,1)} %get-tuple-element.43.w1, bf16[2,3,400,128]{3,2,1,0:T(8,128)(2,1)S(1)} %get-tuple-element.44.w2, ...), custom_call_target="tpu_custom_call" | custom-call | flops 2621440000 | bytes 11000000 | tf_op jit(solution)/shard_map/cond/branch_1_fun/late/pallas_call | solution.py:235
  95.5 7.9 %collective-permute-start.9 = (bf16[32,160,128]{2,1,0:T(8,128)(2,1)S(1)}, bf16[32,160,128]{2,1,0:T(8,128)(2,1)S(1)}, u32[]{:S(2)}, u32[]{:S(2)}) collective-permute-start(bf16[32,160,128]{2,1,0:T(8,128)(2,1)S(1)} %get-tuple-element.59), channel_id=1, source_target_pairs={{0,1},{1,0},{2,3},{3,2},{4,5},{5,4},{6,7},{7,6},{8,9},{9,8},{10,11... | collective-permute-start | bytes 3932168 | tf_op jit(solution)/shard_map/ppermute | solution.py:317
  103.3 2.6 %collective-permute-done.9 = bf16[32,160,128]{2,1,0:T(8,128)(2,1)S(1)} collective-permute-done((bf16[32,160,128]{2,1,0:T(8,128)(2,1)S(1)}, bf16[32,160,128]{2,1,0:T(8,128)(2,1)S(1)}, u32[]{:S(2)}, u32[]{:S(2)}) %collective-permute-start.9) | collective-permute-done | bytes 1310752 | tf_op jit(solution)/shard_map/ppermute | solution.py:317
  106.0 0.3 add_convert_fusion
  106.3 38.7 %all_to_all.11.in_ref = bf16[32,160,128]{2,1,0:T(8,128)(2,1)S(1)} all-to-all(bf16[32,160,128]{2,1,0:T(8,128)(2,1)S(1)} %add_convert_fusion), channel_id=1, replica_groups=mesh['x'=4,'zh'=4,'yn'=2,'yt'=2,'zl'=4,'core'=2] {'x','yn','zl'}, dimensions={0} | all-to-all | bytes 2621440 | tf_op jit(solution)/shard_map/all_to_all | solution.py:319
  145.0 1.4 add_up.1
  (12 shorter events, 0.2 us)
Async XLA Ops:
  0.0 10.9 %copy-start.4 = (bf16[1,25,3200]{2,1,0:T(8,128)(2,1)S(1)}, bf16[1,25,3200]{2,1,0:T(8,128)(2,1)}, u32[]{:S(2)}) copy-start(bf16[1,25,3200]{2,1,0:T(8,128)(2,1)} %param.8) | copy-start | bytes 480004
  5.3 17.7 %collective-permute-start.4 = (bf16[3,400,128]{2,1,0:T(8,128)(2,1)S(1)}, bf16[3,400,128]{2,1,0:T(8,128)(2,1)S(1)}, u32[]{:S(2)}, u32[]{:S(2)}) collective-permute-start(bf16[3,400,128]{2,1,0:T(8,128)(2,1)S(1)} %squeeze.3), channel_id=1, source_target_pairs={{0,16},{16,0},{1,17},{17,1},{2,18},{18,2},{3,19},{19,3},{4,20},{20... | collective-permute-start | bytes 921608 | tf_op jit(solution)/shard_map/ppermute | solution.py:308
  23.1 51.9 %copy-start.5 = (s32[9]{0:T(128)S(1)}, s32[9]{0:T(128)}, u32[]{:S(2)}) copy-start(s32[9]{0:T(128)} %param.11) | copy-start | bytes 112
  23.1 53.3 %collective-permute-start.8 = (bf16[2,3,400,128]{3,2,1,0:T(8,128)(2,1)S(1)}, bf16[2,3,400,128]{3,2,1,0:T(8,128)(2,1)S(1)}, u32[]{:S(2)}, u32[]{:S(2)}) collective-permute-start(bf16[2,3,400,128]{3,2,1,0:T(8,128)(2,1)S(1)} %pad_maximum_fusion.1.w0), channel_id=1, source_target_pairs={{0,128},{128,256},{256,384},{384,0},{1,129},{129,257},{257,385},{3... | collective-permute-start | bytes 1843208 | tf_op jit(solution)/shard_map/ppermute | solution.py:287
  25.0 51.4 %collective-permute-start.7 = (bf16[2,3,400,128]{3,2,1,0:T(8,128)(2,1)S(1)}, bf16[2,3,400,128]{3,2,1,0:T(8,128)(2,1)S(1)}, u32[]{:S(2)}, u32[]{:S(2)}) collective-permute-start(bf16[2,3,400,128]{3,2,1,0:T(8,128)(2,1)S(1)} %pad_maximum_fusion.1.w0), channel_id=1, source_target_pairs={{0,256},{128,384},{256,0},{384,128},{1,257},{129,385},{257,1},{385... | collective-permute-start | bytes 1843208 | tf_op jit(solution)/shard_map/ppermute | solution.py:287
  28.9 47.5 %collective-permute-start.6 = (bf16[2,3,400,128]{3,2,1,0:T(8,128)(2,1)S(1)}, bf16[2,3,400,128]{3,2,1,0:T(8,128)(2,1)}, u32[]{:S(2)}, u32[]{:S(2)}) collective-permute-start(bf16[2,3,400,128]{3,2,1,0:T(8,128)(2,1)S(1)} %pad_maximum_fusion.1.w0), channel_id=1, source_target_pairs={{0,384},{128,0},{256,128},{384,256},{1,385},{129,1},{257,129},{385... | collective-permute-start | bytes 1843208 | tf_op jit(solution)/shard_map/ppermute | solution.py:287
  71.6 14.7 %collective-permute-start.5 = (bf16[4,100,800]{2,0,1:T(4,128)(2,1)}, bf16[4,100,800]{2,0,1:T(4,128)(2,1)S(1)}, u32[]{:S(2)}, u32[]{:S(2)}) collective-permute-start(bf16[4,100,800]{2,0,1:T(4,128)(2,1)} %copy.14), channel_id=1, source_target_pairs={{0,8},{8,0},{1,9},{9,1},{2,10},{10,2},{3,11},{11,3},{4,12},{12,4},... | collective-permute-start | bytes 1920008 | tf_op jit(solution)/shard_map/ppermute | solution.py:314
  76.4 9.9 %copy-start.3 = (bf16[50,100,128]{2,1,0:T(8,128)(2,1)S(1)}, bf16[50,100,128]{2,1,0:T(8,128)(2,1)}, u32[]{:S(2)}) copy-start(bf16[50,100,128]{2,1,0:T(8,128)(2,1)} %v_ref.1) | copy-start | bytes 3840004
  95.5 10.5 %collective-permute-start.9 = (bf16[32,160,128]{2,1,0:T(8,128)(2,1)S(1)}, bf16[32,160,128]{2,1,0:T(8,128)(2,1)S(1)}, u32[]{:S(2)}, u32[]{:S(2)}) collective-permute-start(bf16[32,160,128]{2,1,0:T(8,128)(2,1)S(1)} %get-tuple-element.59), channel_id=1, source_target_pairs={{0,1},{1,0},{2,3},{3,2},{4,5},{5,4},{6,7},{7,6},{8,9},{9,8},{10,11... | collective-permute-start | bytes 3932168 | tf_op jit(solution)/shard_map/ppermute | solution.py:317

commit v4 on v3

--- a/solution.py
+++ b/solution.py
@@ -11,6 +11,8 @@
 A_ROW = 8
 B_DEV = 50
 D_DEV = 100
+D_ROW = 25
+CHUNK = 80
 N_DEV = 400
 GROUPS = 8
 ROWS = A_ROW * B_DEV
@@ -113,16 +115,52 @@
     )(table, v)
 
 
-def fill_rows(tp, t):
-    tp[...] = jnp.zeros_like(tp)
-    for z in range(4):
-        block = t[z].astype(jnp.float32)
-        for h in range(2):
-            part = block[:, h * N_DEV:(h + 1) * N_DEV].astype(jnp.bfloat16)
-            tp[pl.ds((2 * z + h) * KB, D_DEV), :] = part
-
-
-def fill_labels(table, a_labels, bd_labels):
+def pack_kernel(t_ref, out_ref, rows, tail):
+    rows[...] = jnp.zeros_like(rows)
+    tail[...] = jnp.zeros_like(tail)
+    for g in range(GROUPS):
+        block = t_ref[0, :, g * N_DEV:(g + 1) * N_DEV].astype(jnp.float32)
+        for s in range(TILES):
+            rows[pl.ds(g * CHUNK + s * D_ROW, D_ROW), :] = block[:, s * KB:(s + 1) * KB]
+        tail[pl.ds(0, D_ROW), pl.ds(0, LEFT)] = block[:, TILES * KB:]
+        left = tail[pl.ds(0, 4, stride=8), :]
+        for s in range(1, 8):
+            left = left + pltpu.roll(tail[pl.ds(s, 4, stride=8), :], LEFT * s, 1)
+        rows[pl.ds(g * CHUNK + TILES * D_ROW, 4), :] = left
+    out_ref[...] = rows[...].astype(jnp.bfloat16)
+
+
+def pack(t):
+    vmem = pl.BlockSpec(memory_space=pltpu.VMEM)
+    return pl.pallas_call(
+        pack_kernel,
+        in_specs=[vmem],
+        out_specs=vmem,
+        out_shape=jax.ShapeDtypeStruct((GROUPS * CHUNK, KB), jnp.bfloat16),
+        scratch_shapes=[pltpu.VMEM((GROUPS * CHUNK, KB), jnp.float32), pltpu.VMEM((32, KB), jnp.float32)],
+        compiler_params=pltpu.CompilerParams(vmem_limit_bytes=8 * 2**20),
+        name="pack",
+    )(t)
+
+
+def fill_rows(tp, t, block, tail):
+    block[...] = jnp.zeros_like(block)
+
+    @pl.loop(0, CB // 2)
+    def _(i):
+        for x in range(4):
+            start = pl.multiple_of(((i >> 1) * GROUPS + 2 * x + (i & 1)) * CHUNK, 16)
+            chunk = t[pl.ds(start, CHUNK), :].astype(jnp.float32)
+            for s in range(TILES):
+                block[pl.ds(x * D_ROW, D_ROW), pl.ds(s * KB, KB)] = chunk[s * D_ROW:(s + 1) * D_ROW]
+            left = chunk[TILES * D_ROW:TILES * D_ROW + 4]
+            for s in range(8):
+                tail[x, pl.ds(s, 4, stride=8), :] = left if s == 0 else pltpu.roll(left, KB - LEFT * s, 1)
+            block[pl.ds(x * D_ROW, D_ROW), pl.ds(TILES * KB, LEFT)] = tail[x, pl.ds(0, D_ROW), pl.ds(0, LEFT)]
+        tp[pl.ds(pl.multiple_of(i * KB, KB), KB), :] = block[...].astype(jnp.bfloat16)
+
+
+def fill_labels(table, base, a_labels):
     place, a_off, v_off, _ = parts_of(table)
     row = lax.broadcasted_iota(jnp.int32, (ROWS, KB), 0)
     lane = lax.broadcasted_iota(jnp.int32, (ROWS, KB), 1)
@@ -130,8 +168,13 @@
     d_label = count_at_or_above(lane + place[1], v_off)
     for s in range(4):
         a_labels[s] = count_at_or_above(a + s * A_ROW, a_off)
-    for s in range(2):
-        bd_labels[s] = d_label ^ count_at_or_above(row - a * B_DEV + place[0] + s * 2 * B_DEV, v_off)
+    for h in range(2):
+        first = place[0] + yn_at(h, table) * 2 * B_DEV
+        bd_label = d_label ^ count_at_or_above(row - a * B_DEV + first, v_off)
+
+        @pl.loop(0, 4)
+        def _(j):
+            base[j, h] = (bd_label ^ a_labels[x_at(2 * j, table)]).astype(jnp.float32).astype(jnp.bfloat16)
 
 
 def x_at(step, table):
@@ -142,114 +185,98 @@
     return table[7] ^ (step & 1)
 
 
-def product(table, step, w_ref, yt, tp, a_labels, bd_labels):
+def product(table, j, w_ref, yt, tp, base):
     c_off = parts_of(table)[3]
-    base = (a_labels[x_at(step, table)] ^ bd_labels[yn_at(step, table)]).astype(jnp.float32).astype(jnp.bfloat16)
-    masked = []
-    for z in range(4):
-        for h in range(2):
-            c = 4 * z + 2 * h + yt
+    halves = []
+    for h in range(2):
+        labels = base[j, h]
+        masked = []
+        for i in range(CB // 2):
+            c = 2 * i + yt
             c_label = count_at_or_above(c, c_off)
-            rank = jnp.minimum(c - c_off[c_label], w_ref.shape[1] - 1)
-            w = w_ref[step & 1, rank]
-            hit = base == c_label.astype(jnp.float32).astype(jnp.bfloat16)
+            rank = jnp.minimum(c - c_off[c_label], w_ref.shape[2] - 1)
+            w = w_ref[j, h, rank]
+            hit = labels == c_label.astype(jnp.float32).astype(jnp.bfloat16)
             masked.append(jnp.where(hit, w, jnp.zeros_like(w)))
-    return jnp.dot(jnp.concatenate(masked, axis=1), tp[...], preferred_element_type=jnp.float32)
-
-
-def early_kernel(table, w0, w1, w2, w3, t, out_ref, tp, a_labels, bd_labels):
-    step = pl.program_id(0)
-
-    @pl.when(step == 0)
-    def _():
-        fill_rows(tp, t)
-        fill_labels(table, a_labels, bd_labels)
-
-    for j, w in enumerate((w0, w1, w2, w3)):
-        @pl.when(step >> 1 == j)
-        def _(w=w):
-            out_ref[0] = product(table, step, w, table[3], tp, a_labels, bd_labels)
-
-
-def late_kernel(table, w0, w1, w2, w3, t, part_ref, mine_ref, other_ref, tp, a_labels, bd_labels, acc, tail, packed):
-    step = pl.program_id(0)
-
-    @pl.when(step == 0)
-    def _():
-        fill_rows(tp, t)
-        fill_labels(table, a_labels, bd_labels)
-        tail[...] = jnp.zeros_like(tail)
-        packed[...] = jnp.zeros_like(packed)
-
-    for j, w in enumerate((w0, w1, w2, w3)):
-        @pl.when(step >> 1 == j)
-        def _(w=w):
-            acc[...] = part_ref[0] + product(table, step, w, 1 - table[3], tp, a_labels, bd_labels)
-
-    tail[pl.ds(0, ROWS), pl.ds(0, LEFT)] = acc[:, TILES * KB:]
-    for a in range(A_ROW):
-        for s in range(TILES):
-            packed[a, pl.ds(8 + s * B_DEV, B_DEV), :] = acc[a * B_DEV:(a + 1) * B_DEV, s * KB:(s + 1) * KB]
-        left = tail[pl.ds(a * B_DEV, 8, stride=8), :]
-        for s in range(1, 8):
-            left = left + pltpu.roll(tail[pl.ds(a * B_DEV + s, 8, stride=8), :], LEFT * s, 1)
-        packed[a, pl.ds(0, 8), :] = left
-    for z in range(4):
-        mine_ref[z] = packed[2 * z + table[4]].astype(jnp.bfloat16)
-        other_ref[z] = packed[2 * z + 1 - table[4]].astype(jnp.bfloat16)
+        halves.append(jnp.concatenate(masked, axis=1))
+    return jnp.dot(jnp.concatenate(halves, axis=0), tp[...], preferred_element_type=jnp.float32)
+
+
+def early_kernel(table, w_ref, t, out_ref, base, tp, block, tail, a_labels):
+    fill_rows(tp, t, block, tail)
+    fill_labels(table, base, a_labels)
+
+    @pl.loop(0, 4)
+    def _(j):
+        out_ref[j] = product(table, j, w_ref, table[3], tp, base)
+
+
+def late_kernel(table, w_ref, t, part_ref, base, mine_ref, other_ref, tp, block, tail, acc, side, packed):
+    fill_rows(tp, t, block, tail)
+    side[...] = jnp.zeros_like(side)
+    packed[...] = jnp.zeros_like(packed)
+
+    @pl.loop(0, 4)
+    def _(j):
+        acc[...] = part_ref[j] + product(table, j, w_ref, 1 - table[3], tp, base)
+
+        @pl.loop(0, 2)
+        def _(h):
+            part = acc.at[pl.ds(pl.multiple_of(h * ROWS, 8), ROWS)]
+            side[pl.ds(0, ROWS), pl.ds(0, LEFT)] = part[:, TILES * KB:]
+            for a in range(A_ROW):
+                for s in range(TILES):
+                    packed[a, pl.ds(8 + s * B_DEV, B_DEV), :] = part[a * B_DEV:(a + 1) * B_DEV, s * KB:(s + 1) * KB]
+                left = side[pl.ds(a * B_DEV, 8, stride=8), :]
+                for s in range(1, 8):
+                    left = left + pltpu.roll(side[pl.ds(a * B_DEV + s, 8, stride=8), :], LEFT * s, 1)
+                packed[a, pl.ds(0, 8), :] = left
+            to = 4 * (2 * x_at(2 * j, table) + yn_at(h, table))
+            for z in range(4):
+                mine_ref[to + z] = packed[2 * z + table[4]].astype(jnp.bfloat16)
+                other_ref[to + z] = packed[2 * z + 1 - table[4]].astype(jnp.bfloat16)
 
 
 SCRATCH = [
     pltpu.VMEM((CB // 2 * KB, N_DEV), jnp.bfloat16),
-    pltpu.VMEM((4, ROWS, KB), jnp.int32),
-    pltpu.VMEM((2, ROWS, KB), jnp.int32),
+    pltpu.VMEM((KB, N_DEV), jnp.float32),
+    pltpu.VMEM((4, 32, KB), jnp.float32),
 ]
-PART = pl.BlockSpec((1, ROWS, N_DEV), lambda i, tab: (i, 0, 0))
-
-
-def operands(ranks):
-    w_spec = pl.BlockSpec((2, ranks, ROWS, KB), lambda i, tab: (0, 0, 0, 0))
-    return [w_spec] * 4 + [pl.BlockSpec((4, D_DEV, 2 * N_DEV), lambda i, tab: (0, 0, 0))]
-
-
-def early(table, ws, t):
+VMEM = pl.BlockSpec(memory_space=pltpu.VMEM)
+
+
+def early(table, w, t):
     return pl.pallas_call(
         early_kernel,
-        grid_spec=pltpu.PrefetchScalarGridSpec(
-            num_scalar_prefetch=1,
-            grid=(GROUPS,),
-            in_specs=operands(ws[0].shape[1]),
-            out_specs=PART,
-            scratch_shapes=SCRATCH,
-        ),
-        out_shape=jax.ShapeDtypeStruct((GROUPS, ROWS, N_DEV), jnp.float32),
-        compiler_params=pltpu.CompilerParams(vmem_limit_bytes=50 * 2**20),
+        in_specs=[SMEM] + [VMEM] * 2,
+        out_specs=[VMEM, VMEM],
+        out_shape=[
+            jax.ShapeDtypeStruct((4, 2 * ROWS, N_DEV), jnp.float32),
+            jax.ShapeDtypeStruct((4, 2, ROWS, KB), jnp.bfloat16),
+        ],
+        scratch_shapes=SCRATCH + [pltpu.VMEM((4, ROWS, KB), jnp.int32)],
+        compiler_params=pltpu.CompilerParams(vmem_limit_bytes=32 * 2**20),
         cost_estimate=pl.CostEstimate(flops=2 * 3200 * 1024 * 400, bytes_accessed=9000000, transcendentals=0),
         name="early",
-    )(table, *ws, t)
-
-
-def late(table, ws, t, partial):
-    o_spec = pl.BlockSpec((4, PACKED, KB), lambda i, tab: (2 * x_at(i, tab) + yn_at(i, tab), 0, 0))
+    )(table, w, t)
+
+
+def late(table, w, t, partial, base):
     o_shape = jax.ShapeDtypeStruct((4 * GROUPS, PACKED, KB), jnp.bfloat16)
     return pl.pallas_call(
         late_kernel,
-        grid_spec=pltpu.PrefetchScalarGridSpec(
-            num_scalar_prefetch=1,
-            grid=(GROUPS,),
-            in_specs=operands(ws[0].shape[1]) + [PART],
-            out_specs=[o_spec, o_spec],
-            scratch_shapes=SCRATCH + [
-                pltpu.VMEM((ROWS, N_DEV), jnp.float32),
-                pltpu.VMEM((ROWS + 16, KB), jnp.float32),
-                pltpu.VMEM((A_ROW, PACKED, KB), jnp.float32),
-            ],
-        ),
+        in_specs=[SMEM] + [VMEM] * 4,
+        out_specs=[VMEM, VMEM],
         out_shape=[o_shape, o_shape],
-        compiler_params=pltpu.CompilerParams(vmem_limit_bytes=50 * 2**20),
+        scratch_shapes=SCRATCH + [
+            pltpu.VMEM((2 * ROWS, N_DEV), jnp.float32),
+            pltpu.VMEM((ROWS + 16, KB), jnp.float32),
+            pltpu.VMEM((A_ROW, PACKED, KB), jnp.float32),
+        ],
+        compiler_params=pltpu.CompilerParams(vmem_limit_bytes=32 * 2**20),
         cost_estimate=pl.CostEstimate(flops=2 * 3200 * 1024 * 400, bytes_accessed=11000000, transcendentals=0),
         name="late",
-    )(table, *ws, t, partial)
+    )(table, w, t, partial, base)
 
 
 def add_kernel(in_ref, out_ref, tail, rows):
@@ -284,17 +311,17 @@
 
 
 def around(w):
-    return [w] + [lax.ppermute(w, "x", turn(k)) for k in (1, 2, 3)]
-
-
-def again(table, integrals, ws, own, beside, partial):
+    return jnp.stack([w] + [lax.ppermute(w, "x", turn(k)) for k in (1, 2, 3)])
+
+
+def again(table, integrals, w, own, beside, *done):
     w = squeeze(RANKS_MOST, table, integrals)
-    ws = around(jnp.stack([w, lax.ppermute(w, "yn", SWAP)]))
-    return late(table, ws, beside, early(table, ws, own))
-
-
-def finish(table, integrals, ws, own, beside, partial):
-    return late(table, ws, beside, partial)
+    w = around(jnp.stack([w, lax.ppermute(w, "yn", SWAP)]))
+    return late(table, w, beside, *early(table, w, own))
+
+
+def finish(table, integrals, w, own, beside, *done):
+    return late(table, w, beside, *done)
 
 
 def shards(integrals, amplitudes, a_offsets, vir_offsets, c_offsets):
@@ -306,14 +333,12 @@
     narrow = jnp.max(c_offsets[1:] - c_offsets[:-1]) <= RANKS_FEW
     w = squeeze(RANKS_FEW, table, integrals)
     w_beside = lax.ppermute(w, "yn", SWAP)
-    t = lax.all_to_all(amplitudes.reshape(25, GROUPS, N_DEV).transpose(1, 0, 2), ("x", "yn"), 0, 0, tiled=True)
-    t = t.reshape(4, 2, 25, N_DEV).transpose(0, 2, 1, 3).reshape(1, D_DEV, 2 * N_DEV)
+    t = lax.all_to_all(pack(amplitudes), ("x", "yn"), 0, 0, tiled=True)
     t, w, w_beside = lax.optimization_barrier((t, w, w_beside))
-    ws = around(jnp.stack([w, w_beside]))
+    w = around(jnp.stack([w, w_beside]))
     own = lax.all_gather(t, "zh", axis=0, tiled=True)
     beside = lax.ppermute(own, "yt", SWAP)
-    partial = early(table, ws, own)
-    mine, other = lax.cond(narrow, finish, again, table, integrals, ws, own, beside, partial)
+    mine, other = lax.cond(narrow, finish, again, table, integrals, w, own, beside, *early(table, w, own))
     got = lax.ppermute(other, "core", SWAP)
     total = (mine.astype(f32) + got.astype(f32)).astype(bf16)
     return add_up(lax.all_to_all(total, ("x", "yn", "zl"), 0, 0, tiled=True))

time: 147 us -> 138 us (0.939)
  Pallas kernels: 22.6 us -> 19.5 us
  starting transfers between devices: 25.9 us -> 22.8 us
  blocking collectives: 88.1 us -> 85.3 us
  local copies, waits for them, and re-layouts: 2.99 us -> 0.82 us
  other arithmetic: 1.1 us -> 2.78 us
    all_gather x1, blocking collectives: 38.3 us -> 34.3 us  [shards(): own = lax.all_gather(t, 'zh', axis=0, tiled=True)]
    pallas_call x2 -> x3, Pallas kernels: 16.7 us -> 13.6 us  [the longest x1 7.05 us: late(): pl.pallas_call(late_kernel, in_specs=[SMEM] + [VMEM] * 4, out_specs=[VMEM...]
    another operation x1 -> x2, other arithmetic: 0.06 us -> 1.65 us  [around(): return jnp.stack([w] + [lax.ppermute(w, 'x', turn(k)) for k in (1, 2, 3)])]
where the time goes in v4:
time: 138 us; the launch traced here: 137 us
  blocking collectives  85.3 us (62%)
  starting transfers between devices  22.8 us (17%)
  Pallas kernels  19.5 us (14%)
  waiting for transfers between devices  5.43 us (4%)
  other arithmetic  2.78 us (2%)
    all_to_all x1, blocking collectives, shards(): return add_up(lax.all_to_all(total, ('x', 'yn', 'zl'), 0, 0, tiled=True))  40.2 us
    all_gather x1, blocking collectives, shards(): own = lax.all_gather(t, 'zh', axis=0, tiled=True)  34.3 us
    all_to_all x1, blocking collectives, shards(): t = lax.all_to_all(pack(amplitudes), ('x', 'yn'), 0, 0, tiled=True)  10.8 us
    ppermute x3, starting transfers between devices, around(): return jnp.stack([w] + [lax.ppermute(w, 'x', turn(k)) for k in (1, 2, 3)])  8.27 us
    pallas_call x1, Pallas kernels, late(): pl.pallas_call(late_kernel, in_specs=[SMEM] + [VMEM] * 4, out_specs=[VMEM...  7.05 us
    ppermute x1, starting transfers between devices, shards(): got = lax.ppermute(other, 'core', SWAP)  6.55 us
    pallas_call x1, Pallas kernels, early(): pl.pallas_call(early_kernel, in_specs=[SMEM] + [VMEM] * 2, out_specs=[VME...  6.29 us
    ppermute x1, starting transfers between devices, shards(): w_beside = lax.ppermute(w, 'yn', SWAP)  5.65 us
  transfers between devices with their start and end apart: 6, of which 2 were waited for; matrix products, arithmetic and copies ran while one was open for 2% of the time, Pallas kernels for 5%

profile of v4, /device:TPU:1, one launch (start us, length us, event | category | flops | bytes accessed | tf_op | source)
XLA Modules:
  0.0 137.4 jit_solution(16737354023036173888)
XLA Ops:
  0.0 0.8 concatenate.3.table
  0.8 4.5 %squeeze.3 = bf16[3,400,128]{2,1,0:T(8,128)(2,1)S(1)} custom-call(s32[35]{0:T(128)S(1)} %concatenate.3.table, bf16[50,100,128]{2,1,0:T(8,128)(2,1)} %v_ref.1), custom_call_target="tpu_custom_call" | custom-call | flops 30720000 | bytes 2400000 | tf_op jit(solution)/shard_map/squeeze/pallas_call | solution.py:105
  5.3 0.0 copy-start.2
  5.3 5.7 %collective-permute-start.4 = (bf16[3,400,128]{2,1,0:T(8,128)(2,1)S(1)}, bf16[3,400,128]{2,1,0:T(8,128)(2,1)S(1)}, u32[]{:S(2)}, u32[]{:S(2)}) collective-permute-start(bf16[3,400,128]{2,1,0:T(8,128)(2,1)S(1)} %squeeze.3), channel_id=1, source_target_pairs={{0,16},{16,0},{1,17},{17,1},{2,18},{18,2},{3,19},{19,3},{4,20},{20... | collective-permute-start | bytes 921608 | tf_op jit(solution)/shard_map/ppermute | solution.py:335
  11.0 0.3 pack.1
  11.2 10.8 %all_to_all.17 = bf16[8,80,128]{2,1,0:T(8,128)(2,1)S(1)} all-to-all(bf16[8,80,128]{2,1,0:T(8,128)(2,1)S(1)} %bitcast.26), channel_id=1, replica_groups=mesh['x'=4,'zh'=4,'yn'=2,'yt'=2,'zl'=4,'core'=2] {'x','yn'}, dimensions={0} | all-to-all | bytes 327680 | tf_op jit(solution)/shard_map/all_to_all | solution.py:336
  22.1 0.1 fusion.1
  22.1 3.0 %collective-permute-start.7 = (bf16[2,3,400,128]{3,2,1,0:T(8,128)(2,1)S(1)}, bf16[2,3,400,128]{3,2,1,0:T(8,128)(2,1)S(1)}, u32[]{:S(2)}, u32[]{:S(2)}) collective-permute-start(bf16[2,3,400,128]{3,2,1,0:T(8,128)(2,1)S(1)} %get-tuple-element.63), channel_id=1, source_target_pairs={{0,256},{128,384},{256,0},{384,128},{1,257},{129,385},{257,1},{385... | collective-permute-start | bytes 1843208 | tf_op jit(solution)/shard_map/ppermute | solution.py:314
  25.1 3.3 %collective-permute-start.6 = (bf16[2,3,400,128]{3,2,1,0:T(8,128)(2,1)S(1)}, bf16[2,3,400,128]{3,2,1,0:T(8,128)(2,1)}, u32[]{:S(2)}, u32[]{:S(2)}) collective-permute-start(bf16[2,3,400,128]{3,2,1,0:T(8,128)(2,1)S(1)} %get-tuple-element.63), channel_id=1, source_target_pairs={{0,384},{128,0},{256,128},{384,256},{1,385},{129,1},{257,129},{385... | collective-permute-start | bytes 1843208 | tf_op jit(solution)/shard_map/ppermute | solution.py:314
  28.4 2.0 %collective-permute-start.8 = (bf16[2,3,400,128]{3,2,1,0:T(8,128)(2,1)S(1)}, bf16[2,3,400,128]{3,2,1,0:T(8,128)(2,1)}, u32[]{:S(2)}, u32[]{:S(2)}) collective-permute-start(bf16[2,3,400,128]{3,2,1,0:T(8,128)(2,1)S(1)} %get-tuple-element.63), channel_id=1, source_target_pairs={{0,128},{128,256},{256,384},{384,0},{1,129},{129,257},{257,385},{3... | collective-permute-start | bytes 1843208 | tf_op jit(solution)/shard_map/ppermute | solution.py:314
  30.4 34.3 %all_gather.3.t = bf16[2560,128]{1,0:T(8,128)(2,1)S(1)} all-gather(bf16[640,128]{1,0:T(8,128)(2,1)S(1)} %bitcast.31), channel_id=1, replica_groups=mesh['x'=4,'zh'=4,'yn'=2,'yt'=2,'zl'=4,'core'=2] {'zh'}, dimensions={0}, use_global_device_ids=true | all-gather | bytes 819200 | tf_op jit(solution)/shard_map/all_gather | solution.py:339
  64.7 2.3 %collective-permute-start.5 = (bf16[2560,128]{1,0:T(8,128)(2,1)S(1)}, bf16[2560,128]{1,0:T(8,128)(2,1)S(1)}, u32[]{:S(2)}, u32[]{:S(2)}) collective-permute-start(bf16[2560,128]{1,0:T(8,128)(2,1)S(1)} %all_gather.3.t), channel_id=1, source_target_pairs={{0,8},{8,0},{1,9},{9,1},{2,10},{10,2},{3,11},{11,3},{4,12},{12,4},... | collective-permute-start | bytes 1966088 | tf_op jit(solution)/shard_map/ppermute | solution.py:340
  67.1 0.7 subtract_reduce_fusion
  68.5 1.6 %pad_maximum_fusion.2.w_ref = bf16[4,2,3,400,128]{4,3,2,1,0:T(8,128)(2,1)S(1)} fusion(bf16[1,2,3,400,128]{4,3,2,1,0:T(8,128)(2,1)} %bitcast.21, bf16[1,2,3,400,128]{4,3,2,1,0:T(8,128)(2,1)S(1)} %bitcast.32, bf16[1,2,3,400,128]{4,3,2,1,0:T(8,128)(2,1)} %bitcast.19, bf16[1,2,3,400,128]{4,3,2,1,0:T(8,128)(2,1)S(1)} %get-tuple-element.62), kind=kLoop, calls=%fused_computation.4 | loop fusion | flops 3686400 | bytes 4915200 | tf_op jit(solution)/shard_map/stack | solution.py:314
  70.0 0.0 copy-start.1
  70.1 6.3 %early.3 = (f32[4,800,400]{2,1,0:T(8,128)S(1)}, bf16[4,2,400,128]{3,2,1,0:T(8,128)(2,1)S(1)}) custom-call(s32[35]{0:T(128)S(1)} %concatenate.3.table, bf16[4,2,3,400,128]{4,3,2,1,0:T(8,128)(2,1)S(1)} %pad_maximum_fusion.2.w_ref, bf16[2560,128]{1,0:T(8,128)(2,1)S(1)} %all_gather.3.t), custom_call_target="tpu_custom_call" | custom-call | flops 2621440000 | bytes 9000000 | tf_op jit(solution)/shard_map/early/pallas_call | solution.py:249
  76.4 2.8 %collective-permute-done.5 = bf16[2560,128]{1,0:T(8,128)(2,1)S(1)} collective-permute-done((bf16[2560,128]{1,0:T(8,128)(2,1)S(1)}, bf16[2560,128]{1,0:T(8,128)(2,1)S(1)}, u32[]{:S(2)}, u32[]{:S(2)}) %collective-permute-start.5) | collective-permute-done | bytes 655392 | tf_op jit(solution)/shard_map/ppermute | solution.py:340
  79.1 7.1 %conditional.2 = (bf16[32,160,128]{2,1,0:T(8,128)(2,1)S(1)}, bf16[32,160,128]{2,1,0:T(8,128)(2,1)S(1)}) conditional(s32[]{:T(128)} %convert_element_type.15, (s32[35]{0:T(128)S(1)}, bf16[50,100,128]{2,1,0:T(8,128)(2,1)S(1)}, bf16[2560,128]{1,0:T(8,128)(2,1)S(1)}, bf16[2560,128]{1,0:T(8,128)(2,1)S(1)}) %tuple.26, (s32[35]{0:T(128)S(1)}, ...), branch_computations={%region_1.0_spmd, %region_2.0_spmd} | conditional | flops 5347020800 | bytes 68480176
  79.1 7.0 %late.3 = (bf16[32,160,128]{2,1,0:T(8,128)(2,1)S(1)}, bf16[32,160,128]{2,1,0:T(8,128)(2,1)S(1)}) custom-call(s32[35]{0:T(128)S(1)} %get-tuple-element.39.table, bf16[4,2,3,400,128]{4,3,2,1,0:T(8,128)(2,1)S(1)} %get-tuple-element.40.w_ref, bf16[2560,128]{1,0:T(8,128)(2,1)S(1)} %get-tuple-element.41.t, f32[4,800,400]{2,1,0:T(8,128)S(1)} %get-tuple-element.42.part_ref, ...), custom_call_target="tpu_custom_call" | custom-call | flops 2621440000 | bytes 11000000 | tf_op jit(solution)/shard_map/cond/branch_1_fun/late/pallas_call | solution.py:266
  86.2 6.5 %collective-permute-start.9 = (bf16[32,160,128]{2,1,0:T(8,128)(2,1)S(1)}, bf16[32,160,128]{2,1,0:T(8,128)(2,1)S(1)}, u32[]{:S(2)}, u32[]{:S(2)}) collective-permute-start(bf16[32,160,128]{2,1,0:T(8,128)(2,1)S(1)} %get-tuple-element.59), channel_id=1, source_target_pairs={{0,1},{1,0},{2,3},{3,2},{4,5},{5,4},{6,7},{7,6},{8,9},{9,8},{10,11... | collective-permute-start | bytes 3932168 | tf_op jit(solution)/shard_map/ppermute | solution.py:342
  92.7 2.6 %collective-permute-done.9 = bf16[32,160,128]{2,1,0:T(8,128)(2,1)S(1)} collective-permute-done((bf16[32,160,128]{2,1,0:T(8,128)(2,1)S(1)}, bf16[32,160,128]{2,1,0:T(8,128)(2,1)S(1)}, u32[]{:S(2)}, u32[]{:S(2)}) %collective-permute-start.9) | collective-permute-done | bytes 1310752 | tf_op jit(solution)/shard_map/ppermute | solution.py:342
  95.4 0.4 add_convert_fusion
  95.8 40.2 %all_to_all.18.in_ref = bf16[32,160,128]{2,1,0:T(8,128)(2,1)S(1)} all-to-all(bf16[32,160,128]{2,1,0:T(8,128)(2,1)S(1)} %add_convert_fusion), channel_id=1, replica_groups=mesh['x'=4,'zh'=4,'yn'=2,'yt'=2,'zl'=4,'core'=2] {'x','yn','zl'}, dimensions={0} | all-to-all | bytes 2621440 | tf_op jit(solution)/shard_map/all_to_all | solution.py:344
  136.0 1.4 %add_up.1 = bf16[1,50,3200]{2,1,0:T(8,128)(2,1)} custom-call(bf16[32,160,128]{2,1,0:T(8,128)(2,1)S(1)} %all_to_all.18.in_ref), custom_call_target="tpu_custom_call" | custom-call | tf_op jit(solution)/shard_map/add_up/pallas_call | solution.py:298
  (8 shorter events, 0.0 us)
Async XLA Ops:
  0.0 10.9 %copy-start = (bf16[1,25,3200]{2,1,0:T(8,128)(2,1)S(1)}, bf16[1,25,3200]{2,1,0:T(8,128)(2,1)}, u32[]{:S(2)}) copy-start(bf16[1,25,3200]{2,1,0:T(8,128)(2,1)} %t_ref.1) | copy-start | bytes 480004
  5.3 61.8 %copy-start.2 = (s32[9]{0:T(128)S(1)}, s32[9]{0:T(128)}, u32[]{:S(2)}) copy-start(s32[9]{0:T(128)} %param.11) | copy-start | bytes 112
  5.3 16.8 %collective-permute-start.4 = (bf16[3,400,128]{2,1,0:T(8,128)(2,1)S(1)}, bf16[3,400,128]{2,1,0:T(8,128)(2,1)S(1)}, u32[]{:S(2)}, u32[]{:S(2)}) collective-permute-start(bf16[3,400,128]{2,1,0:T(8,128)(2,1)S(1)} %squeeze.3), channel_id=1, source_target_pairs={{0,16},{16,0},{1,17},{17,1},{2,18},{18,2},{3,19},{19,3},{4,20},{20... | collective-permute-start | bytes 921608 | tf_op jit(solution)/shard_map/ppermute | solution.py:335
  22.1 46.3 %collective-permute-start.7 = (bf16[2,3,400,128]{3,2,1,0:T(8,128)(2,1)S(1)}, bf16[2,3,400,128]{3,2,1,0:T(8,128)(2,1)S(1)}, u32[]{:S(2)}, u32[]{:S(2)}) collective-permute-start(bf16[2,3,400,128]{3,2,1,0:T(8,128)(2,1)S(1)} %get-tuple-element.63), channel_id=1, source_target_pairs={{0,256},{128,384},{256,0},{384,128},{1,257},{129,385},{257,1},{385... | collective-permute-start | bytes 1843208 | tf_op jit(solution)/shard_map/ppermute | solution.py:314
  25.1 43.3 %collective-permute-start.6 = (bf16[2,3,400,128]{3,2,1,0:T(8,128)(2,1)S(1)}, bf16[2,3,400,128]{3,2,1,0:T(8,128)(2,1)}, u32[]{:S(2)}, u32[]{:S(2)}) collective-permute-start(bf16[2,3,400,128]{3,2,1,0:T(8,128)(2,1)S(1)} %get-tuple-element.63), channel_id=1, source_target_pairs={{0,384},{128,0},{256,128},{384,256},{1,385},{129,1},{257,129},{385... | collective-permute-start | bytes 1843208 | tf_op jit(solution)/shard_map/ppermute | solution.py:314
  28.4 40.1 %collective-permute-start.8 = (bf16[2,3,400,128]{3,2,1,0:T(8,128)(2,1)S(1)}, bf16[2,3,400,128]{3,2,1,0:T(8,128)(2,1)}, u32[]{:S(2)}, u32[]{:S(2)}) collective-permute-start(bf16[2,3,400,128]{3,2,1,0:T(8,128)(2,1)S(1)} %get-tuple-element.63), channel_id=1, source_target_pairs={{0,128},{128,256},{256,384},{384,0},{1,129},{129,257},{257,385},{3... | collective-permute-start | bytes 1843208 | tf_op jit(solution)/shard_map/ppermute | solution.py:314
  64.7 14.4 %collective-permute-start.5 = (bf16[2560,128]{1,0:T(8,128)(2,1)S(1)}, bf16[2560,128]{1,0:T(8,128)(2,1)S(1)}, u32[]{:S(2)}, u32[]{:S(2)}) collective-permute-start(bf16[2560,128]{1,0:T(8,128)(2,1)S(1)} %all_gather.3.t), channel_id=1, source_target_pairs={{0,8},{8,0},{1,9},{9,1},{2,10},{10,2},{3,11},{11,3},{4,12},{12,4},... | collective-permute-start | bytes 1966088 | tf_op jit(solution)/shard_map/ppermute | solution.py:340
  70.0 9.1 %copy-start.1 = (bf16[50,100,128]{2,1,0:T(8,128)(2,1)S(1)}, bf16[50,100,128]{2,1,0:T(8,128)(2,1)}, u32[]{:S(2)}) copy-start(bf16[50,100,128]{2,1,0:T(8,128)(2,1)} %v_ref.1) | copy-start | bytes 3840004
  86.2 9.2 %collective-permute-start.9 = (bf16[32,160,128]{2,1,0:T(8,128)(2,1)S(1)}, bf16[32,160,128]{2,1,0:T(8,128)(2,1)S(1)}, u32[]{:S(2)}, u32[]{:S(2)}) collective-permute-start(bf16[32,160,128]{2,1,0:T(8,128)(2,1)S(1)} %get-tuple-element.59), channel_id=1, source_target_pairs={{0,1},{1,0},{2,3},{3,2},{4,5},{5,4},{6,7},{7,6},{8,9},{9,8},{10,11... | collective-permute-start | bytes 3932168 | tf_op jit(solution)/shard_map/ppermute | solution.py:342

commit v5 on v4

--- a/solution.py
+++ b/solution.py
@@ -101,7 +101,7 @@
 
 
 def squeeze(ranks, table, v):
-    b_step = 10
+    b_step = B_DEV
     return pl.pallas_call(
         functools.partial(squeeze_kernel, ranks),
         grid=(B_DEV // b_step,),

time: 138 us -> 136 us (0.986)
  Pallas kernels: 19.5 us -> 17.7 us
    pallas_call x1, Pallas kernels: 4.46 us -> 2.69 us  [squeeze(): pl.pallas_call(functools.partial(squeeze_kernel, ranks), grid=(B_DEV // b...]
where the time goes in v5:
time: 136 us
  blocking collectives  85.3 us (63%)
  starting transfers between devices  23.6 us (17%)
  Pallas kernels  17.7 us (13%)
  waiting for transfers between devices  4.63 us (3%)
  other arithmetic  2.78 us (2%)
    all_to_all x1, blocking collectives, shards(): return add_up(lax.all_to_all(total, ('x', 'yn', 'zl'), 0, 0, tiled=True))  40.6 us
    all_gather x1, blocking collectives, shards(): own = lax.all_gather(t, 'zh', axis=0, tiled=True)  33.9 us
    all_to_all x1, blocking collectives, shards(): t = lax.all_to_all(pack(amplitudes), ('x', 'yn'), 0, 0, tiled=True)  10.8 us
    ppermute x3, starting transfers between devices, around(): return jnp.stack([w] + [lax.ppermute(w, 'x', turn(k)) for k in (1, 2, 3)])  8.27 us
    pallas_call x1, Pallas kernels, late(): pl.pallas_call(late_kernel, in_specs=[SMEM] + [VMEM] * 4, out_specs=[VMEM...  7.03 us
    ppermute x1, starting transfers between devices, shards(): got = lax.ppermute(other, 'core', SWAP)  6.9 us
    pallas_call x1, Pallas kernels, early(): pl.pallas_call(early_kernel, in_specs=[SMEM] + [VMEM] * 2, out_specs=[VME...  6.29 us
    ppermute x1, starting transfers between devices, shards(): w_beside = lax.ppermute(w, 'yn', SWAP)  5.65 us
  transfers between devices with their start and end apart: 6, of which 2 were waited for; matrix products, arithmetic and copies ran while one was open for 2% of the time, Pallas kernels for 5%

profile of v5, /device:TPU:1, one launch (start us, length us, event | category | flops | bytes accessed | tf_op | source)
XLA Modules:
  0.0 135.6 jit_solution(17712174986904238879)
XLA Ops:
  0.0 0.8 concatenate.3.table
  0.8 2.7 %squeeze.3 = bf16[3,400,128]{2,1,0:T(8,128)(2,1)S(1)} custom-call(s32[35]{0:T(128)S(1)} %concatenate.3.table, bf16[50,100,128]{2,1,0:T(8,128)(2,1)} %v_ref.1), custom_call_target="tpu_custom_call" | custom-call | flops 30720000 | bytes 2400000 | tf_op jit(solution)/shard_map/squeeze/pallas_call | solution.py:105
  3.5 0.0 copy-start.2
  3.5 5.7 %collective-permute-start.4 = (bf16[3,400,128]{2,1,0:T(8,128)(2,1)S(1)}, bf16[3,400,128]{2,1,0:T(8,128)(2,1)S(1)}, u32[]{:S(2)}, u32[]{:S(2)}) collective-permute-start(bf16[3,400,128]{2,1,0:T(8,128)(2,1)S(1)} %squeeze.3), channel_id=1, source_target_pairs={{0,16},{16,0},{1,17},{17,1},{2,18},{18,2},{3,19},{19,3},{4,20},{20... | collective-permute-start | bytes 921608 | tf_op jit(solution)/shard_map/ppermute | solution.py:335
  9.2 0.3 pack.1
  9.5 10.8 %all_to_all.17 = bf16[8,80,128]{2,1,0:T(8,128)(2,1)S(1)} all-to-all(bf16[8,80,128]{2,1,0:T(8,128)(2,1)S(1)} %bitcast.26), channel_id=1, replica_groups=mesh['x'=4,'zh'=4,'yn'=2,'yt'=2,'zl'=4,'core'=2] {'x','yn'}, dimensions={0} | all-to-all | bytes 327680 | tf_op jit(solution)/shard_map/all_to_all | solution.py:336
  20.3 0.1 fusion.1
  20.4 3.0 %collective-permute-start.7 = (bf16[2,3,400,128]{3,2,1,0:T(8,128)(2,1)S(1)}, bf16[2,3,400,128]{3,2,1,0:T(8,128)(2,1)S(1)}, u32[]{:S(2)}, u32[]{:S(2)}) collective-permute-start(bf16[2,3,400,128]{3,2,1,0:T(8,128)(2,1)S(1)} %get-tuple-element.63), channel_id=1, source_target_pairs={{0,256},{128,384},{256,0},{384,128},{1,257},{129,385},{257,1},{385... | collective-permute-start | bytes 1843208 | tf_op jit(solution)/shard_map/ppermute | solution.py:314
  23.4 3.3 %collective-permute-start.6 = (bf16[2,3,400,128]{3,2,1,0:T(8,128)(2,1)S(1)}, bf16[2,3,400,128]{3,2,1,0:T(8,128)(2,1)}, u32[]{:S(2)}, u32[]{:S(2)}) collective-permute-start(bf16[2,3,400,128]{3,2,1,0:T(8,128)(2,1)S(1)} %get-tuple-element.63), channel_id=1, source_target_pairs={{0,384},{128,0},{256,128},{384,256},{1,385},{129,1},{257,129},{385... | collective-permute-start | bytes 1843208 | tf_op jit(solution)/shard_map/ppermute | solution.py:314
  26.6 2.0 %collective-permute-start.8 = (bf16[2,3,400,128]{3,2,1,0:T(8,128)(2,1)S(1)}, bf16[2,3,400,128]{3,2,1,0:T(8,128)(2,1)}, u32[]{:S(2)}, u32[]{:S(2)}) collective-permute-start(bf16[2,3,400,128]{3,2,1,0:T(8,128)(2,1)S(1)} %get-tuple-element.63), channel_id=1, source_target_pairs={{0,128},{128,256},{256,384},{384,0},{1,129},{129,257},{257,385},{3... | collective-permute-start | bytes 1843208 | tf_op jit(solution)/shard_map/ppermute | solution.py:314
  28.7 33.9 %all_gather.3.t = bf16[2560,128]{1,0:T(8,128)(2,1)S(1)} all-gather(bf16[640,128]{1,0:T(8,128)(2,1)S(1)} %bitcast.31), channel_id=1, replica_groups=mesh['x'=4,'zh'=4,'yn'=2,'yt'=2,'zl'=4,'core'=2] {'zh'}, dimensions={0}, use_global_device_ids=true | all-gather | bytes 819200 | tf_op jit(solution)/shard_map/all_gather | solution.py:339
  62.5 2.8 %collective-permute-start.5 = (bf16[2560,128]{1,0:T(8,128)(2,1)S(1)}, bf16[2560,128]{1,0:T(8,128)(2,1)S(1)}, u32[]{:S(2)}, u32[]{:S(2)}) collective-permute-start(bf16[2560,128]{1,0:T(8,128)(2,1)S(1)} %all_gather.3.t), channel_id=1, source_target_pairs={{0,8},{8,0},{1,9},{9,1},{2,10},{10,2},{3,11},{11,3},{4,12},{12,4},... | collective-permute-start | bytes 1966088 | tf_op jit(solution)/shard_map/ppermute | solution.py:340
  65.3 0.7 subtract_reduce_fusion
  66.7 1.6 %pad_maximum_fusion.2.w_ref = bf16[4,2,3,400,128]{4,3,2,1,0:T(8,128)(2,1)S(1)} fusion(bf16[1,2,3,400,128]{4,3,2,1,0:T(8,128)(2,1)} %bitcast.21, bf16[1,2,3,400,128]{4,3,2,1,0:T(8,128)(2,1)S(1)} %bitcast.32, bf16[1,2,3,400,128]{4,3,2,1,0:T(8,128)(2,1)} %bitcast.19, bf16[1,2,3,400,128]{4,3,2,1,0:T(8,128)(2,1)S(1)} %get-tuple-element.62), kind=kLoop, calls=%fused_computation.4 | loop fusion | flops 3686400 | bytes 4915200 | tf_op jit(solution)/shard_map/stack | solution.py:314
  68.3 0.0 copy-start.1
  68.3 6.3 %early.3 = (f32[4,800,400]{2,1,0:T(8,128)S(1)}, bf16[4,2,400,128]{3,2,1,0:T(8,128)(2,1)S(1)}) custom-call(s32[35]{0:T(128)S(1)} %concatenate.3.table, bf16[4,2,3,400,128]{4,3,2,1,0:T(8,128)(2,1)S(1)} %pad_maximum_fusion.2.w_ref, bf16[2560,128]{1,0:T(8,128)(2,1)S(1)} %all_gather.3.t), custom_call_target="tpu_custom_call" | custom-call | flops 2621440000 | bytes 9000000 | tf_op jit(solution)/shard_map/early/pallas_call | solution.py:249
  74.6 2.0 %collective-permute-done.5 = bf16[2560,128]{1,0:T(8,128)(2,1)S(1)} collective-permute-done((bf16[2560,128]{1,0:T(8,128)(2,1)S(1)}, bf16[2560,128]{1,0:T(8,128)(2,1)S(1)}, u32[]{:S(2)}, u32[]{:S(2)}) %collective-permute-start.5) | collective-permute-done | bytes 655392 | tf_op jit(solution)/shard_map/ppermute | solution.py:340
  76.6 7.0 %conditional.2 = (bf16[32,160,128]{2,1,0:T(8,128)(2,1)S(1)}, bf16[32,160,128]{2,1,0:T(8,128)(2,1)S(1)}) conditional(s32[]{:T(128)} %convert_element_type.15, (s32[35]{0:T(128)S(1)}, bf16[50,100,128]{2,1,0:T(8,128)(2,1)S(1)}, bf16[2560,128]{1,0:T(8,128)(2,1)S(1)}, bf16[2560,128]{1,0:T(8,128)(2,1)S(1)}) %tuple.26, (s32[35]{0:T(128)S(1)}, ...), branch_computations={%region_1.0_spmd, %region_2.0_spmd} | conditional | flops 5347020800 | bytes 68480176
  76.6 7.0 %late.3 = (bf16[32,160,128]{2,1,0:T(8,128)(2,1)S(1)}, bf16[32,160,128]{2,1,0:T(8,128)(2,1)S(1)}) custom-call(s32[35]{0:T(128)S(1)} %get-tuple-element.39.table, bf16[4,2,3,400,128]{4,3,2,1,0:T(8,128)(2,1)S(1)} %get-tuple-element.40.w_ref, bf16[2560,128]{1,0:T(8,128)(2,1)S(1)} %get-tuple-element.41.t, f32[4,800,400]{2,1,0:T(8,128)S(1)} %get-tuple-element.42.part_ref, ...), custom_call_target="tpu_custom_call" | custom-call | flops 2621440000 | bytes 11000000 | tf_op jit(solution)/shard_map/cond/branch_1_fun/late/pallas_call | solution.py:266
  83.6 6.9 %collective-permute-start.9 = (bf16[32,160,128]{2,1,0:T(8,128)(2,1)S(1)}, bf16[32,160,128]{2,1,0:T(8,128)(2,1)S(1)}, u32[]{:S(2)}, u32[]{:S(2)}) collective-permute-start(bf16[32,160,128]{2,1,0:T(8,128)(2,1)S(1)} %get-tuple-element.59), channel_id=1, source_target_pairs={{0,1},{1,0},{2,3},{3,2},{4,5},{5,4},{6,7},{7,6},{8,9},{9,8},{10,11... | collective-permute-start | bytes 3932168 | tf_op jit(solution)/shard_map/ppermute | solution.py:342
  90.5 2.6 %collective-permute-done.9 = bf16[32,160,128]{2,1,0:T(8,128)(2,1)S(1)} collective-permute-done((bf16[32,160,128]{2,1,0:T(8,128)(2,1)S(1)}, bf16[32,160,128]{2,1,0:T(8,128)(2,1)S(1)}, u32[]{:S(2)}, u32[]{:S(2)}) %collective-permute-start.9) | collective-permute-done | bytes 1310752 | tf_op jit(solution)/shard_map/ppermute | solution.py:342
  93.2 0.4 add_convert_fusion
  93.6 40.6 %all_to_all.18.in_ref = bf16[32,160,128]{2,1,0:T(8,128)(2,1)S(1)} all-to-all(bf16[32,160,128]{2,1,0:T(8,128)(2,1)S(1)} %add_convert_fusion), channel_id=1, replica_groups=mesh['x'=4,'zh'=4,'yn'=2,'yt'=2,'zl'=4,'core'=2] {'x','yn','zl'}, dimensions={0} | all-to-all | bytes 2621440 | tf_op jit(solution)/shard_map/all_to_all | solution.py:344
  134.2 1.4 %add_up.1 = bf16[1,50,3200]{2,1,0:T(8,128)(2,1)} custom-call(bf16[32,160,128]{2,1,0:T(8,128)(2,1)S(1)} %all_to_all.18.in_ref), custom_call_target="tpu_custom_call" | custom-call | tf_op jit(solution)/shard_map/add_up/pallas_call | solution.py:298
  (8 shorter events, 0.0 us)
Async XLA Ops:
  0.0 9.2 %copy-start = (bf16[1,25,3200]{2,1,0:T(8,128)(2,1)S(1)}, bf16[1,25,3200]{2,1,0:T(8,128)(2,1)}, u32[]{:S(2)}) copy-start(bf16[1,25,3200]{2,1,0:T(8,128)(2,1)} %t_ref.1) | copy-start | bytes 480004
  3.5 61.8 %copy-start.2 = (s32[9]{0:T(128)S(1)}, s32[9]{0:T(128)}, u32[]{:S(2)}) copy-start(s32[9]{0:T(128)} %param.11) | copy-start | bytes 112
  3.5 16.8 %collective-permute-start.4 = (bf16[3,400,128]{2,1,0:T(8,128)(2,1)S(1)}, bf16[3,400,128]{2,1,0:T(8,128)(2,1)S(1)}, u32[]{:S(2)}, u32[]{:S(2)}) collective-permute-start(bf16[3,400,128]{2,1,0:T(8,128)(2,1)S(1)} %squeeze.3), channel_id=1, source_target_pairs={{0,16},{16,0},{1,17},{17,1},{2,18},{18,2},{3,19},{19,3},{4,20},{20... | collective-permute-start | bytes 921608 | tf_op jit(solution)/shard_map/ppermute | solution.py:335
  20.4 46.3 %collective-permute-start.7 = (bf16[2,3,400,128]{3,2,1,0:T(8,128)(2,1)S(1)}, bf16[2,3,400,128]{3,2,1,0:T(8,128)(2,1)S(1)}, u32[]{:S(2)}, u32[]{:S(2)}) collective-permute-start(bf16[2,3,400,128]{3,2,1,0:T(8,128)(2,1)S(1)} %get-tuple-element.63), channel_id=1, source_target_pairs={{0,256},{128,384},{256,0},{384,128},{1,257},{129,385},{257,1},{385... | collective-permute-start | bytes 1843208 | tf_op jit(solution)/shard_map/ppermute | solution.py:314
  23.4 43.3 %collective-permute-start.6 = (bf16[2,3,400,128]{3,2,1,0:T(8,128)(2,1)S(1)}, bf16[2,3,400,128]{3,2,1,0:T(8,128)(2,1)}, u32[]{:S(2)}, u32[]{:S(2)}) collective-permute-start(bf16[2,3,400,128]{3,2,1,0:T(8,128)(2,1)S(1)} %get-tuple-element.63), channel_id=1, source_target_pairs={{0,384},{128,0},{256,128},{384,256},{1,385},{129,1},{257,129},{385... | collective-permute-start | bytes 1843208 | tf_op jit(solution)/shard_map/ppermute | solution.py:314
  26.6 40.1 %collective-permute-start.8 = (bf16[2,3,400,128]{3,2,1,0:T(8,128)(2,1)S(1)}, bf16[2,3,400,128]{3,2,1,0:T(8,128)(2,1)}, u32[]{:S(2)}, u32[]{:S(2)}) collective-permute-start(bf16[2,3,400,128]{3,2,1,0:T(8,128)(2,1)S(1)} %get-tuple-element.63), channel_id=1, source_target_pairs={{0,128},{128,256},{256,384},{384,0},{1,129},{129,257},{257,385},{3... | collective-permute-start | bytes 1843208 | tf_op jit(solution)/shard_map/ppermute | solution.py:314
  62.5 14.0 %collective-permute-start.5 = (bf16[2560,128]{1,0:T(8,128)(2,1)S(1)}, bf16[2560,128]{1,0:T(8,128)(2,1)S(1)}, u32[]{:S(2)}, u32[]{:S(2)}) collective-permute-start(bf16[2560,128]{1,0:T(8,128)(2,1)S(1)} %all_gather.3.t), channel_id=1, source_target_pairs={{0,8},{8,0},{1,9},{9,1},{2,10},{10,2},{3,11},{11,3},{4,12},{12,4},... | collective-permute-start | bytes 1966088 | tf_op jit(solution)/shard_map/ppermute | solution.py:340
  68.3 8.3 %copy-start.1 = (bf16[50,100,128]{2,1,0:T(8,128)(2,1)S(1)}, bf16[50,100,128]{2,1,0:T(8,128)(2,1)}, u32[]{:S(2)}) copy-start(bf16[50,100,128]{2,1,0:T(8,128)(2,1)} %v_ref.1) | copy-start | bytes 3840004
  83.6 9.5 %collective-permute-start.9 = (bf16[32,160,128]{2,1,0:T(8,128)(2,1)S(1)}, bf16[32,160,128]{2,1,0:T(8,128)(2,1)S(1)}, u32[]{:S(2)}, u32[]{:S(2)}) collective-permute-start(bf16[32,160,128]{2,1,0:T(8,128)(2,1)S(1)} %get-tuple-element.59), channel_id=1, source_target_pairs={{0,1},{1,0},{2,3},{3,2},{4,5},{5,4},{6,7},{7,6},{8,9},{9,8},{10,11... | collective-permute-start | bytes 3932168 | tf_op jit(solution)/shard_map/ppermute | solution.py:342

commit v6 on v5

--- a/solution.py
+++ b/solution.py
@@ -137,7 +137,7 @@
         in_specs=[vmem],
         out_specs=vmem,
         out_shape=jax.ShapeDtypeStruct((GROUPS * CHUNK, KB), jnp.bfloat16),
-        scratch_shapes=[pltpu.VMEM((GROUPS * CHUNK, KB), jnp.float32), pltpu.VMEM((32, KB), jnp.float32)],
+        scratch_shapes=[pltpu.VMEM((GROUPS * CHUNK, KB), jnp.float32), pltpu.VMEM((40, KB), jnp.float32)],
         compiler_params=pltpu.CompilerParams(vmem_limit_bytes=8 * 2**20),
         name="pack",
     )(t)
@@ -240,7 +240,7 @@
 SCRATCH = [
     pltpu.VMEM((CB // 2 * KB, N_DEV), jnp.bfloat16),
     pltpu.VMEM((KB, N_DEV), jnp.float32),
-    pltpu.VMEM((4, 32, KB), jnp.float32),
+    pltpu.VMEM((4, 40, KB), jnp.float32),
 ]
 VMEM = pl.BlockSpec(memory_space=pltpu.VMEM)
 
@@ -270,7 +270,7 @@
         out_shape=[o_shape, o_shape],
         scratch_shapes=SCRATCH + [
             pltpu.VMEM((2 * ROWS, N_DEV), jnp.float32),
-            pltpu.VMEM((ROWS + 16, KB), jnp.float32),
+            pltpu.VMEM((ROWS + 32, KB), jnp.float32),
             pltpu.VMEM((A_ROW, PACKED, KB), jnp.float32),
         ],
         compiler_params=pltpu.CompilerParams(vmem_limit_bytes=32 * 2**20),
@@ -300,7 +300,7 @@
         in_specs=[vmem],
         out_specs=vmem,
         out_shape=jax.ShapeDtypeStruct((1, B_DEV, GROUPS * N_DEV), jnp.bfloat16),
-        scratch_shapes=[pltpu.VMEM((64, KB), jnp.float32), pltpu.VMEM((B_DEV, GROUPS * N_DEV), jnp.float32)],
+        scratch_shapes=[pltpu.VMEM((72, KB), jnp.float32), pltpu.VMEM((B_DEV, GROUPS * N_DEV), jnp.float32)],
         compiler_params=pltpu.CompilerParams(vmem_limit_bytes=20 * 2**20),
         name="add_up",
     )(parts)

time: 136 us -> 136 us (level)
  no operation moved by 1% of the time
where the time goes in v6:
time: 136 us
  blocking collectives  85.3 us (63%)
  starting transfers between devices  23.6 us (17%)
  Pallas kernels  17.7 us (13%)
  waiting for transfers between devices  4.62 us (3%)
  other arithmetic  2.78 us (2%)
    all_to_all x1, blocking collectives, shards(): return add_up(lax.all_to_all(total, ('x', 'yn', 'zl'), 0, 0, tiled=True))  40.6 us
    all_gather x1, blocking collectives, shards(): own = lax.all_gather(t, 'zh', axis=0, tiled=True)  33.9 us
    all_to_all x1, blocking collectives, shards(): t = lax.all_to_all(pack(amplitudes), ('x', 'yn'), 0, 0, tiled=True)  10.8 us
    ppermute x3, starting transfers between devices, around(): return jnp.stack([w] + [lax.ppermute(w, 'x', turn(k)) for k in (1, 2, 3)])  8.27 us
    pallas_call x1, Pallas kernels, late(): pl.pallas_call(late_kernel, in_specs=[SMEM] + [VMEM] * 4, out_specs=[VMEM...  7.06 us
    ppermute x1, starting transfers between devices, shards(): got = lax.ppermute(other, 'core', SWAP)  6.9 us
    pallas_call x1, Pallas kernels, early(): pl.pallas_call(early_kernel, in_specs=[SMEM] + [VMEM] * 2, out_specs=[VME...  6.3 us
    ppermute x1, starting transfers between devices, shards(): w_beside = lax.ppermute(w, 'yn', SWAP)  5.65 us
  transfers between devices with their start and end apart: 6, of which 2 were waited for; matrix products, arithmetic and copies ran while one was open for 2% of the time, Pallas kernels for 5%

profile of v6, /device:TPU:1, one launch (start us, length us, event | category | flops | bytes accessed | tf_op | source)
XLA Modules:
  0.0 135.6 jit_solution(17010957798920425889)
XLA Ops:
  0.0 0.8 concatenate.3.table
  0.8 2.7 %squeeze.3 = bf16[3,400,128]{2,1,0:T(8,128)(2,1)S(1)} custom-call(s32[35]{0:T(128)S(1)} %concatenate.3.table, bf16[50,100,128]{2,1,0:T(8,128)(2,1)} %v_ref.1), custom_call_target="tpu_custom_call" | custom-call | flops 30720000 | bytes 2400000 | tf_op jit(solution)/shard_map/squeeze/pallas_call | solution.py:105
  3.5 0.0 copy-start.2
  3.5 5.7 %collective-permute-start.4 = (bf16[3,400,128]{2,1,0:T(8,128)(2,1)S(1)}, bf16[3,400,128]{2,1,0:T(8,128)(2,1)S(1)}, u32[]{:S(2)}, u32[]{:S(2)}) collective-permute-start(bf16[3,400,128]{2,1,0:T(8,128)(2,1)S(1)} %squeeze.3), channel_id=1, source_target_pairs={{0,16},{16,0},{1,17},{17,1},{2,18},{18,2},{3,19},{19,3},{4,20},{20... | collective-permute-start | bytes 921608 | tf_op jit(solution)/shard_map/ppermute | solution.py:335
  9.2 0.3 pack.1
  9.5 10.8 %all_to_all.17 = bf16[8,80,128]{2,1,0:T(8,128)(2,1)S(1)} all-to-all(bf16[8,80,128]{2,1,0:T(8,128)(2,1)S(1)} %bitcast.26), channel_id=1, replica_groups=mesh['x'=4,'zh'=4,'yn'=2,'yt'=2,'zl'=4,'core'=2] {'x','yn'}, dimensions={0} | all-to-all | bytes 327680 | tf_op jit(solution)/shard_map/all_to_all | solution.py:336
  20.3 0.1 fusion.1
  20.4 3.0 %collective-permute-start.7 = (bf16[2,3,400,128]{3,2,1,0:T(8,128)(2,1)S(1)}, bf16[2,3,400,128]{3,2,1,0:T(8,128)(2,1)S(1)}, u32[]{:S(2)}, u32[]{:S(2)}) collective-permute-start(bf16[2,3,400,128]{3,2,1,0:T(8,128)(2,1)S(1)} %get-tuple-element.63), channel_id=1, source_target_pairs={{0,256},{128,384},{256,0},{384,128},{1,257},{129,385},{257,1},{385... | collective-permute-start | bytes 1843208 | tf_op jit(solution)/shard_map/ppermute | solution.py:314
  23.4 3.3 %collective-permute-start.6 = (bf16[2,3,400,128]{3,2,1,0:T(8,128)(2,1)S(1)}, bf16[2,3,400,128]{3,2,1,0:T(8,128)(2,1)}, u32[]{:S(2)}, u32[]{:S(2)}) collective-permute-start(bf16[2,3,400,128]{3,2,1,0:T(8,128)(2,1)S(1)} %get-tuple-element.63), channel_id=1, source_target_pairs={{0,384},{128,0},{256,128},{384,256},{1,385},{129,1},{257,129},{385... | collective-permute-start | bytes 1843208 | tf_op jit(solution)/shard_map/ppermute | solution.py:314
  26.6 2.0 %collective-permute-start.8 = (bf16[2,3,400,128]{3,2,1,0:T(8,128)(2,1)S(1)}, bf16[2,3,400,128]{3,2,1,0:T(8,128)(2,1)}, u32[]{:S(2)}, u32[]{:S(2)}) collective-permute-start(bf16[2,3,400,128]{3,2,1,0:T(8,128)(2,1)S(1)} %get-tuple-element.63), channel_id=1, source_target_pairs={{0,128},{128,256},{256,384},{384,0},{1,129},{129,257},{257,385},{3... | collective-permute-start | bytes 1843208 | tf_op jit(solution)/shard_map/ppermute | solution.py:314
  28.7 33.9 %all_gather.3.t = bf16[2560,128]{1,0:T(8,128)(2,1)S(1)} all-gather(bf16[640,128]{1,0:T(8,128)(2,1)S(1)} %bitcast.31), channel_id=1, replica_groups=mesh['x'=4,'zh'=4,'yn'=2,'yt'=2,'zl'=4,'core'=2] {'zh'}, dimensions={0}, use_global_device_ids=true | all-gather | bytes 819200 | tf_op jit(solution)/shard_map/all_gather | solution.py:339
  62.5 2.8 %collective-permute-start.5 = (bf16[2560,128]{1,0:T(8,128)(2,1)S(1)}, bf16[2560,128]{1,0:T(8,128)(2,1)S(1)}, u32[]{:S(2)}, u32[]{:S(2)}) collective-permute-start(bf16[2560,128]{1,0:T(8,128)(2,1)S(1)} %all_gather.3.t), channel_id=1, source_target_pairs={{0,8},{8,0},{1,9},{9,1},{2,10},{10,2},{3,11},{11,3},{4,12},{12,4},... | collective-permute-start | bytes 1966088 | tf_op jit(solution)/shard_map/ppermute | solution.py:340
  65.3 0.7 subtract_reduce_fusion
  66.7 1.6 %pad_maximum_fusion.2.w_ref = bf16[4,2,3,400,128]{4,3,2,1,0:T(8,128)(2,1)S(1)} fusion(bf16[1,2,3,400,128]{4,3,2,1,0:T(8,128)(2,1)} %bitcast.21, bf16[1,2,3,400,128]{4,3,2,1,0:T(8,128)(2,1)S(1)} %bitcast.32, bf16[1,2,3,400,128]{4,3,2,1,0:T(8,128)(2,1)} %bitcast.19, bf16[1,2,3,400,128]{4,3,2,1,0:T(8,128)(2,1)S(1)} %get-tuple-element.62), kind=kLoop, calls=%fused_computation.4 | loop fusion | flops 3686400 | bytes 4915200 | tf_op jit(solution)/shard_map/stack | solution.py:314
  68.3 0.0 copy-start.1
  68.3 6.3 %early.3 = (f32[4,800,400]{2,1,0:T(8,128)S(1)}, bf16[4,2,400,128]{3,2,1,0:T(8,128)(2,1)S(1)}) custom-call(s32[35]{0:T(128)S(1)} %concatenate.3.table, bf16[4,2,3,400,128]{4,3,2,1,0:T(8,128)(2,1)S(1)} %pad_maximum_fusion.2.w_ref, bf16[2560,128]{1,0:T(8,128)(2,1)S(1)} %all_gather.3.t), custom_call_target="tpu_custom_call" | custom-call | flops 2621440000 | bytes 9000000 | tf_op jit(solution)/shard_map/early/pallas_call | solution.py:249
  74.6 2.0 %collective-permute-done.5 = bf16[2560,128]{1,0:T(8,128)(2,1)S(1)} collective-permute-done((bf16[2560,128]{1,0:T(8,128)(2,1)S(1)}, bf16[2560,128]{1,0:T(8,128)(2,1)S(1)}, u32[]{:S(2)}, u32[]{:S(2)}) %collective-permute-start.5) | collective-permute-done | bytes 655392 | tf_op jit(solution)/shard_map/ppermute | solution.py:340
  76.6 7.1 %conditional.2 = (bf16[32,160,128]{2,1,0:T(8,128)(2,1)S(1)}, bf16[32,160,128]{2,1,0:T(8,128)(2,1)S(1)}) conditional(s32[]{:T(128)} %convert_element_type.15, (s32[35]{0:T(128)S(1)}, bf16[50,100,128]{2,1,0:T(8,128)(2,1)S(1)}, bf16[2560,128]{1,0:T(8,128)(2,1)S(1)}, bf16[2560,128]{1,0:T(8,128)(2,1)S(1)}) %tuple.26, (s32[35]{0:T(128)S(1)}, ...), branch_computations={%region_1.0_spmd, %region_2.0_spmd} | conditional | flops 5347020800 | bytes 68480176
  76.6 7.1 %late.3 = (bf16[32,160,128]{2,1,0:T(8,128)(2,1)S(1)}, bf16[32,160,128]{2,1,0:T(8,128)(2,1)S(1)}) custom-call(s32[35]{0:T(128)S(1)} %get-tuple-element.39.table, bf16[4,2,3,400,128]{4,3,2,1,0:T(8,128)(2,1)S(1)} %get-tuple-element.40.w_ref, bf16[2560,128]{1,0:T(8,128)(2,1)S(1)} %get-tuple-element.41.t, f32[4,800,400]{2,1,0:T(8,128)S(1)} %get-tuple-element.42.part_ref, ...), custom_call_target="tpu_custom_call" | custom-call | flops 2621440000 | bytes 11000000 | tf_op jit(solution)/shard_map/cond/branch_1_fun/late/pallas_call | solution.py:266
  83.6 6.9 %collective-permute-start.9 = (bf16[32,160,128]{2,1,0:T(8,128)(2,1)S(1)}, bf16[32,160,128]{2,1,0:T(8,128)(2,1)S(1)}, u32[]{:S(2)}, u32[]{:S(2)}) collective-permute-start(bf16[32,160,128]{2,1,0:T(8,128)(2,1)S(1)} %get-tuple-element.59), channel_id=1, source_target_pairs={{0,1},{1,0},{2,3},{3,2},{4,5},{5,4},{6,7},{7,6},{8,9},{9,8},{10,11... | collective-permute-start | bytes 3932168 | tf_op jit(solution)/shard_map/ppermute | solution.py:342
  90.5 2.6 %collective-permute-done.9 = bf16[32,160,128]{2,1,0:T(8,128)(2,1)S(1)} collective-permute-done((bf16[32,160,128]{2,1,0:T(8,128)(2,1)S(1)}, bf16[32,160,128]{2,1,0:T(8,128)(2,1)S(1)}, u32[]{:S(2)}, u32[]{:S(2)}) %collective-permute-start.9) | collective-permute-done | bytes 1310752 | tf_op jit(solution)/shard_map/ppermute | solution.py:342
  93.2 0.4 add_convert_fusion
  93.6 40.6 %all_to_all.18.in_ref = bf16[32,160,128]{2,1,0:T(8,128)(2,1)S(1)} all-to-all(bf16[32,160,128]{2,1,0:T(8,128)(2,1)S(1)} %add_convert_fusion), channel_id=1, replica_groups=mesh['x'=4,'zh'=4,'yn'=2,'yt'=2,'zl'=4,'core'=2] {'x','yn','zl'}, dimensions={0} | all-to-all | bytes 2621440 | tf_op jit(solution)/shard_map/all_to_all | solution.py:344
  134.2 1.4 %add_up.1 = bf16[1,50,3200]{2,1,0:T(8,128)(2,1)} custom-call(bf16[32,160,128]{2,1,0:T(8,128)(2,1)S(1)} %all_to_all.18.in_ref), custom_call_target="tpu_custom_call" | custom-call | tf_op jit(solution)/shard_map/add_up/pallas_call | solution.py:298
  (8 shorter events, 0.0 us)
Async XLA Ops:
  0.0 9.2 %copy-start = (bf16[1,25,3200]{2,1,0:T(8,128)(2,1)S(1)}, bf16[1,25,3200]{2,1,0:T(8,128)(2,1)}, u32[]{:S(2)}) copy-start(bf16[1,25,3200]{2,1,0:T(8,128)(2,1)} %t_ref.1) | copy-start | bytes 480004
  3.5 61.8 %copy-start.2 = (s32[9]{0:T(128)S(1)}, s32[9]{0:T(128)}, u32[]{:S(2)}) copy-start(s32[9]{0:T(128)} %param.11) | copy-start | bytes 112
  3.5 16.8 %collective-permute-start.4 = (bf16[3,400,128]{2,1,0:T(8,128)(2,1)S(1)}, bf16[3,400,128]{2,1,0:T(8,128)(2,1)S(1)}, u32[]{:S(2)}, u32[]{:S(2)}) collective-permute-start(bf16[3,400,128]{2,1,0:T(8,128)(2,1)S(1)} %squeeze.3), channel_id=1, source_target_pairs={{0,16},{16,0},{1,17},{17,1},{2,18},{18,2},{3,19},{19,3},{4,20},{20... | collective-permute-start | bytes 921608 | tf_op jit(solution)/shard_map/ppermute | solution.py:335
  20.4 46.3 %collective-permute-start.7 = (bf16[2,3,400,128]{3,2,1,0:T(8,128)(2,1)S(1)}, bf16[2,3,400,128]{3,2,1,0:T(8,128)(2,1)S(1)}, u32[]{:S(2)}, u32[]{:S(2)}) collective-permute-start(bf16[2,3,400,128]{3,2,1,0:T(8,128)(2,1)S(1)} %get-tuple-element.63), channel_id=1, source_target_pairs={{0,256},{128,384},{256,0},{384,128},{1,257},{129,385},{257,1},{385... | collective-permute-start | bytes 1843208 | tf_op jit(solution)/shard_map/ppermute | solution.py:314
  23.4 43.3 %collective-permute-start.6 = (bf16[2,3,400,128]{3,2,1,0:T(8,128)(2,1)S(1)}, bf16[2,3,400,128]{3,2,1,0:T(8,128)(2,1)}, u32[]{:S(2)}, u32[]{:S(2)}) collective-permute-start(bf16[2,3,400,128]{3,2,1,0:T(8,128)(2,1)S(1)} %get-tuple-element.63), channel_id=1, source_target_pairs={{0,384},{128,0},{256,128},{384,256},{1,385},{129,1},{257,129},{385... | collective-permute-start | bytes 1843208 | tf_op jit(solution)/shard_map/ppermute | solution.py:314
  26.6 40.1 %collective-permute-start.8 = (bf16[2,3,400,128]{3,2,1,0:T(8,128)(2,1)S(1)}, bf16[2,3,400,128]{3,2,1,0:T(8,128)(2,1)}, u32[]{:S(2)}, u32[]{:S(2)}) collective-permute-start(bf16[2,3,400,128]{3,2,1,0:T(8,128)(2,1)S(1)} %get-tuple-element.63), channel_id=1, source_target_pairs={{0,128},{128,256},{256,384},{384,0},{1,129},{129,257},{257,385},{3... | collective-permute-start | bytes 1843208 | tf_op jit(solution)/shard_map/ppermute | solution.py:314
  62.5 14.0 %collective-permute-start.5 = (bf16[2560,128]{1,0:T(8,128)(2,1)S(1)}, bf16[2560,128]{1,0:T(8,128)(2,1)S(1)}, u32[]{:S(2)}, u32[]{:S(2)}) collective-permute-start(bf16[2560,128]{1,0:T(8,128)(2,1)S(1)} %all_gather.3.t), channel_id=1, source_target_pairs={{0,8},{8,0},{1,9},{9,1},{2,10},{10,2},{3,11},{11,3},{4,12},{12,4},... | collective-permute-start | bytes 1966088 | tf_op jit(solution)/shard_map/ppermute | solution.py:340
  68.3 8.3 %copy-start.1 = (bf16[50,100,128]{2,1,0:T(8,128)(2,1)S(1)}, bf16[50,100,128]{2,1,0:T(8,128)(2,1)}, u32[]{:S(2)}) copy-start(bf16[50,100,128]{2,1,0:T(8,128)(2,1)} %v_ref.1) | copy-start | bytes 3840004
  83.6 9.5 %collective-permute-start.9 = (bf16[32,160,128]{2,1,0:T(8,128)(2,1)S(1)}, bf16[32,160,128]{2,1,0:T(8,128)(2,1)S(1)}, u32[]{:S(2)}, u32[]{:S(2)}) collective-permute-start(bf16[32,160,128]{2,1,0:T(8,128)(2,1)S(1)} %get-tuple-element.59), channel_id=1, source_target_pairs={{0,1},{1,0},{2,3},{3,2},{4,5},{5,4},{6,7},{7,6},{8,9},{9,8},{10,11... | collective-permute-start | bytes 3932168 | tf_op jit(solution)/shard_map/ppermute | solution.py:342

commit v7 on v6

--- a/solution.py
+++ b/solution.py
@@ -109,7 +109,7 @@
         out_specs=pl.BlockSpec((ranks, ROWS, KB), lambda i: (0, 0, 0)),
         out_shape=jax.ShapeDtypeStruct((ranks, ROWS, KB), jnp.bfloat16),
         scratch_shapes=[pltpu.VMEM((ranks, ROWS, KB), jnp.bfloat16)],
-        compiler_params=pltpu.CompilerParams(vmem_limit_bytes=40 * 2**20),
+        compiler_params=pltpu.CompilerParams(vmem_limit_bytes=16 * 2**20),
         cost_estimate=pl.CostEstimate(flops=2 * 5000 * 128 * 8 * ranks, bytes_accessed=2400000, transcendentals=0),
         name="squeeze",
     )(table, v)
@@ -255,7 +255,7 @@
             jax.ShapeDtypeStruct((4, 2, ROWS, KB), jnp.bfloat16),
         ],
         scratch_shapes=SCRATCH + [pltpu.VMEM((4, ROWS, KB), jnp.int32)],
-        compiler_params=pltpu.CompilerParams(vmem_limit_bytes=32 * 2**20),
+        compiler_params=pltpu.CompilerParams(vmem_limit_bytes=16 * 2**20),
         cost_estimate=pl.CostEstimate(flops=2 * 3200 * 1024 * 400, bytes_accessed=9000000, transcendentals=0),
         name="early",
     )(table, w, t)
@@ -273,7 +273,7 @@
             pltpu.VMEM((ROWS + 32, KB), jnp.float32),
             pltpu.VMEM((A_ROW, PACKED, KB), jnp.float32),
         ],
-        compiler_params=pltpu.CompilerParams(vmem_limit_bytes=32 * 2**20),
+        compiler_params=pltpu.CompilerParams(vmem_limit_bytes=16 * 2**20),
         cost_estimate=pl.CostEstimate(flops=2 * 3200 * 1024 * 400, bytes_accessed=11000000, transcendentals=0),
         name="late",
     )(table, w, t, partial, base)

time: 136 us -> 136 us (level)
  no operation moved by 1% of the time
where the time goes in v7:
time: 136 us
  blocking collectives  85.3 us (63%)
  starting transfers between devices  23.6 us (17%)
  Pallas kernels  17.7 us (13%)
  waiting for transfers between devices  4.61 us (3%)
  other arithmetic  2.78 us (2%)
    all_to_all x1, blocking collectives, shards(): return add_up(lax.all_to_all(total, ('x', 'yn', 'zl'), 0, 0, tiled=True))  40.6 us
    all_gather x1, blocking collectives, shards(): own = lax.all_gather(t, 'zh', axis=0, tiled=True)  33.9 us
    all_to_all x1, blocking collectives, shards(): t = lax.all_to_all(pack(amplitudes), ('x', 'yn'), 0, 0, tiled=True)  10.8 us
    ppermute x3, starting transfers between devices, around(): return jnp.stack([w] + [lax.ppermute(w, 'x', turn(k)) for k in (1, 2, 3)])  8.27 us
    pallas_call x1, Pallas kernels, late(): pl.pallas_call(late_kernel, in_specs=[SMEM] + [VMEM] * 4, out_specs=[VMEM...  7.04 us
    ppermute x1, starting transfers between devices, shards(): got = lax.ppermute(other, 'core', SWAP)  6.9 us
    pallas_call x1, Pallas kernels, early(): pl.pallas_call(early_kernel, in_specs=[SMEM] + [VMEM] * 2, out_specs=[VME...  6.31 us
    ppermute x1, starting transfers between devices, shards(): w_beside = lax.ppermute(w, 'yn', SWAP)  5.65 us
  transfers between devices with their start and end apart: 6, of which 2 were waited for; matrix products, arithmetic and copies ran while one was open for 2% of the time, Pallas kernels for 5%

profile of v7, /device:TPU:1, one launch (start us, length us, event | category | flops | bytes accessed | tf_op | source)
XLA Modules:
  0.0 135.6 jit_solution(6064657044941316161)
XLA Ops:
  0.0 0.8 concatenate.3.table
  0.8 2.7 %squeeze.3 = bf16[3,400,128]{2,1,0:T(8,128)(2,1)S(1)} custom-call(s32[35]{0:T(128)S(1)} %concatenate.3.table, bf16[50,100,128]{2,1,0:T(8,128)(2,1)} %v_ref.1), custom_call_target="tpu_custom_call" | custom-call | flops 30720000 | bytes 2400000 | tf_op jit(solution)/shard_map/squeeze/pallas_call | solution.py:105
  3.5 0.0 copy-start.2
  3.5 5.7 %collective-permute-start.4 = (bf16[3,400,128]{2,1,0:T(8,128)(2,1)S(1)}, bf16[3,400,128]{2,1,0:T(8,128)(2,1)S(1)}, u32[]{:S(2)}, u32[]{:S(2)}) collective-permute-start(bf16[3,400,128]{2,1,0:T(8,128)(2,1)S(1)} %squeeze.3), channel_id=1, source_target_pairs={{0,16},{16,0},{1,17},{17,1},{2,18},{18,2},{3,19},{19,3},{4,20},{20... | collective-permute-start | bytes 921608 | tf_op jit(solution)/shard_map/ppermute | solution.py:335
  9.2 0.3 pack.1
  9.5 10.8 %all_to_all.17 = bf16[8,80,128]{2,1,0:T(8,128)(2,1)S(1)} all-to-all(bf16[8,80,128]{2,1,0:T(8,128)(2,1)S(1)} %bitcast.26), channel_id=1, replica_groups=mesh['x'=4,'zh'=4,'yn'=2,'yt'=2,'zl'=4,'core'=2] {'x','yn'}, dimensions={0} | all-to-all | bytes 327680 | tf_op jit(solution)/shard_map/all_to_all | solution.py:336
  20.3 0.1 fusion.1
  20.4 3.0 %collective-permute-start.7 = (bf16[2,3,400,128]{3,2,1,0:T(8,128)(2,1)S(1)}, bf16[2,3,400,128]{3,2,1,0:T(8,128)(2,1)S(1)}, u32[]{:S(2)}, u32[]{:S(2)}) collective-permute-start(bf16[2,3,400,128]{3,2,1,0:T(8,128)(2,1)S(1)} %get-tuple-element.63), channel_id=1, source_target_pairs={{0,256},{128,384},{256,0},{384,128},{1,257},{129,385},{257,1},{385... | collective-permute-start | bytes 1843208 | tf_op jit(solution)/shard_map/ppermute | solution.py:314
  23.4 3.3 %collective-permute-start.6 = (bf16[2,3,400,128]{3,2,1,0:T(8,128)(2,1)S(1)}, bf16[2,3,400,128]{3,2,1,0:T(8,128)(2,1)}, u32[]{:S(2)}, u32[]{:S(2)}) collective-permute-start(bf16[2,3,400,128]{3,2,1,0:T(8,128)(2,1)S(1)} %get-tuple-element.63), channel_id=1, source_target_pairs={{0,384},{128,0},{256,128},{384,256},{1,385},{129,1},{257,129},{385... | collective-permute-start | bytes 1843208 | tf_op jit(solution)/shard_map/ppermute | solution.py:314
  26.6 2.0 %collective-permute-start.8 = (bf16[2,3,400,128]{3,2,1,0:T(8,128)(2,1)S(1)}, bf16[2,3,400,128]{3,2,1,0:T(8,128)(2,1)}, u32[]{:S(2)}, u32[]{:S(2)}) collective-permute-start(bf16[2,3,400,128]{3,2,1,0:T(8,128)(2,1)S(1)} %get-tuple-element.63), channel_id=1, source_target_pairs={{0,128},{128,256},{256,384},{384,0},{1,129},{129,257},{257,385},{3... | collective-permute-start | bytes 1843208 | tf_op jit(solution)/shard_map/ppermute | solution.py:314
  28.7 33.9 %all_gather.3.t = bf16[2560,128]{1,0:T(8,128)(2,1)S(1)} all-gather(bf16[640,128]{1,0:T(8,128)(2,1)S(1)} %bitcast.31), channel_id=1, replica_groups=mesh['x'=4,'zh'=4,'yn'=2,'yt'=2,'zl'=4,'core'=2] {'zh'}, dimensions={0}, use_global_device_ids=true | all-gather | bytes 819200 | tf_op jit(solution)/shard_map/all_gather | solution.py:339
  62.5 2.8 %collective-permute-start.5 = (bf16[2560,128]{1,0:T(8,128)(2,1)S(1)}, bf16[2560,128]{1,0:T(8,128)(2,1)S(1)}, u32[]{:S(2)}, u32[]{:S(2)}) collective-permute-start(bf16[2560,128]{1,0:T(8,128)(2,1)S(1)} %all_gather.3.t), channel_id=1, source_target_pairs={{0,8},{8,0},{1,9},{9,1},{2,10},{10,2},{3,11},{11,3},{4,12},{12,4},... | collective-permute-start | bytes 1966088 | tf_op jit(solution)/shard_map/ppermute | solution.py:340
  65.3 0.7 subtract_reduce_fusion
  66.7 1.6 %pad_maximum_fusion.2.w_ref = bf16[4,2,3,400,128]{4,3,2,1,0:T(8,128)(2,1)S(1)} fusion(bf16[1,2,3,400,128]{4,3,2,1,0:T(8,128)(2,1)} %bitcast.21, bf16[1,2,3,400,128]{4,3,2,1,0:T(8,128)(2,1)S(1)} %bitcast.32, bf16[1,2,3,400,128]{4,3,2,1,0:T(8,128)(2,1)} %bitcast.19, bf16[1,2,3,400,128]{4,3,2,1,0:T(8,128)(2,1)S(1)} %get-tuple-element.62), kind=kLoop, calls=%fused_computation.4 | loop fusion | flops 3686400 | bytes 4915200 | tf_op jit(solution)/shard_map/stack | solution.py:314
  68.3 0.0 copy-start.1
  68.3 6.3 %early.3 = (f32[4,800,400]{2,1,0:T(8,128)S(1)}, bf16[4,2,400,128]{3,2,1,0:T(8,128)(2,1)S(1)}) custom-call(s32[35]{0:T(128)S(1)} %concatenate.3.table, bf16[4,2,3,400,128]{4,3,2,1,0:T(8,128)(2,1)S(1)} %pad_maximum_fusion.2.w_ref, bf16[2560,128]{1,0:T(8,128)(2,1)S(1)} %all_gather.3.t), custom_call_target="tpu_custom_call" | custom-call | flops 2621440000 | bytes 9000000 | tf_op jit(solution)/shard_map/early/pallas_call | solution.py:249
  74.6 2.0 %collective-permute-done.5 = bf16[2560,128]{1,0:T(8,128)(2,1)S(1)} collective-permute-done((bf16[2560,128]{1,0:T(8,128)(2,1)S(1)}, bf16[2560,128]{1,0:T(8,128)(2,1)S(1)}, u32[]{:S(2)}, u32[]{:S(2)}) %collective-permute-start.5) | collective-permute-done | bytes 655392 | tf_op jit(solution)/shard_map/ppermute | solution.py:340
  76.6 7.0 %conditional.2 = (bf16[32,160,128]{2,1,0:T(8,128)(2,1)S(1)}, bf16[32,160,128]{2,1,0:T(8,128)(2,1)S(1)}) conditional(s32[]{:T(128)} %convert_element_type.15, (s32[35]{0:T(128)S(1)}, bf16[50,100,128]{2,1,0:T(8,128)(2,1)S(1)}, bf16[2560,128]{1,0:T(8,128)(2,1)S(1)}, bf16[2560,128]{1,0:T(8,128)(2,1)S(1)}) %tuple.26, (s32[35]{0:T(128)S(1)}, ...), branch_computations={%region_1.0_spmd, %region_2.0_spmd} | conditional | flops 5347020800 | bytes 68480176
  76.6 7.0 %late.3 = (bf16[32,160,128]{2,1,0:T(8,128)(2,1)S(1)}, bf16[32,160,128]{2,1,0:T(8,128)(2,1)S(1)}) custom-call(s32[35]{0:T(128)S(1)} %get-tuple-element.39.table, bf16[4,2,3,400,128]{4,3,2,1,0:T(8,128)(2,1)S(1)} %get-tuple-element.40.w_ref, bf16[2560,128]{1,0:T(8,128)(2,1)S(1)} %get-tuple-element.41.t, f32[4,800,400]{2,1,0:T(8,128)S(1)} %get-tuple-element.42.part_ref, ...), custom_call_target="tpu_custom_call" | custom-call | flops 2621440000 | bytes 11000000 | tf_op jit(solution)/shard_map/cond/branch_1_fun/late/pallas_call | solution.py:266
  83.6 6.9 %collective-permute-start.9 = (bf16[32,160,128]{2,1,0:T(8,128)(2,1)S(1)}, bf16[32,160,128]{2,1,0:T(8,128)(2,1)S(1)}, u32[]{:S(2)}, u32[]{:S(2)}) collective-permute-start(bf16[32,160,128]{2,1,0:T(8,128)(2,1)S(1)} %get-tuple-element.59), channel_id=1, source_target_pairs={{0,1},{1,0},{2,3},{3,2},{4,5},{5,4},{6,7},{7,6},{8,9},{9,8},{10,11... | collective-permute-start | bytes 3932168 | tf_op jit(solution)/shard_map/ppermute | solution.py:342
  90.5 2.6 %collective-permute-done.9 = bf16[32,160,128]{2,1,0:T(8,128)(2,1)S(1)} collective-permute-done((bf16[32,160,128]{2,1,0:T(8,128)(2,1)S(1)}, bf16[32,160,128]{2,1,0:T(8,128)(2,1)S(1)}, u32[]{:S(2)}, u32[]{:S(2)}) %collective-permute-start.9) | collective-permute-done | bytes 1310752 | tf_op jit(solution)/shard_map/ppermute | solution.py:342
  93.2 0.4 add_convert_fusion
  93.6 40.6 %all_to_all.18.in_ref = bf16[32,160,128]{2,1,0:T(8,128)(2,1)S(1)} all-to-all(bf16[32,160,128]{2,1,0:T(8,128)(2,1)S(1)} %add_convert_fusion), channel_id=1, replica_groups=mesh['x'=4,'zh'=4,'yn'=2,'yt'=2,'zl'=4,'core'=2] {'x','yn','zl'}, dimensions={0} | all-to-all | bytes 2621440 | tf_op jit(solution)/shard_map/all_to_all | solution.py:344
  134.2 1.4 %add_up.1 = bf16[1,50,3200]{2,1,0:T(8,128)(2,1)} custom-call(bf16[32,160,128]{2,1,0:T(8,128)(2,1)S(1)} %all_to_all.18.in_ref), custom_call_target="tpu_custom_call" | custom-call | tf_op jit(solution)/shard_map/add_up/pallas_call | solution.py:298
  (8 shorter events, 0.0 us)
Async XLA Ops:
  0.0 9.2 %copy-start = (bf16[1,25,3200]{2,1,0:T(8,128)(2,1)S(1)}, bf16[1,25,3200]{2,1,0:T(8,128)(2,1)}, u32[]{:S(2)}) copy-start(bf16[1,25,3200]{2,1,0:T(8,128)(2,1)} %t_ref.1) | copy-start | bytes 480004
  3.5 61.8 %copy-start.2 = (s32[9]{0:T(128)S(1)}, s32[9]{0:T(128)}, u32[]{:S(2)}) copy-start(s32[9]{0:T(128)} %param.11) | copy-start | bytes 112
  3.5 16.8 %collective-permute-start.4 = (bf16[3,400,128]{2,1,0:T(8,128)(2,1)S(1)}, bf16[3,400,128]{2,1,0:T(8,128)(2,1)S(1)}, u32[]{:S(2)}, u32[]{:S(2)}) collective-permute-start(bf16[3,400,128]{2,1,0:T(8,128)(2,1)S(1)} %squeeze.3), channel_id=1, source_target_pairs={{0,16},{16,0},{1,17},{17,1},{2,18},{18,2},{3,19},{19,3},{4,20},{20... | collective-permute-start | bytes 921608 | tf_op jit(solution)/shard_map/ppermute | solution.py:335
  20.4 46.3 %collective-permute-start.7 = (bf16[2,3,400,128]{3,2,1,0:T(8,128)(2,1)S(1)}, bf16[2,3,400,128]{3,2,1,0:T(8,128)(2,1)S(1)}, u32[]{:S(2)}, u32[]{:S(2)}) collective-permute-start(bf16[2,3,400,128]{3,2,1,0:T(8,128)(2,1)S(1)} %get-tuple-element.63), channel_id=1, source_target_pairs={{0,256},{128,384},{256,0},{384,128},{1,257},{129,385},{257,1},{385... | collective-permute-start | bytes 1843208 | tf_op jit(solution)/shard_map/ppermute | solution.py:314
  23.4 43.3 %collective-permute-start.6 = (bf16[2,3,400,128]{3,2,1,0:T(8,128)(2,1)S(1)}, bf16[2,3,400,128]{3,2,1,0:T(8,128)(2,1)}, u32[]{:S(2)}, u32[]{:S(2)}) collective-permute-start(bf16[2,3,400,128]{3,2,1,0:T(8,128)(2,1)S(1)} %get-tuple-element.63), channel_id=1, source_target_pairs={{0,384},{128,0},{256,128},{384,256},{1,385},{129,1},{257,129},{385... | collective-permute-start | bytes 1843208 | tf_op jit(solution)/shard_map/ppermute | solution.py:314
  26.6 40.1 %collective-permute-start.8 = (bf16[2,3,400,128]{3,2,1,0:T(8,128)(2,1)S(1)}, bf16[2,3,400,128]{3,2,1,0:T(8,128)(2,1)}, u32[]{:S(2)}, u32[]{:S(2)}) collective-permute-start(bf16[2,3,400,128]{3,2,1,0:T(8,128)(2,1)S(1)} %get-tuple-element.63), channel_id=1, source_target_pairs={{0,128},{128,256},{256,384},{384,0},{1,129},{129,257},{257,385},{3... | collective-permute-start | bytes 1843208 | tf_op jit(solution)/shard_map/ppermute | solution.py:314
  62.5 14.0 %collective-permute-start.5 = (bf16[2560,128]{1,0:T(8,128)(2,1)S(1)}, bf16[2560,128]{1,0:T(8,128)(2,1)S(1)}, u32[]{:S(2)}, u32[]{:S(2)}) collective-permute-start(bf16[2560,128]{1,0:T(8,128)(2,1)S(1)} %all_gather.3.t), channel_id=1, source_target_pairs={{0,8},{8,0},{1,9},{9,1},{2,10},{10,2},{3,11},{11,3},{4,12},{12,4},... | collective-permute-start | bytes 1966088 | tf_op jit(solution)/shard_map/ppermute | solution.py:340
  68.3 8.3 %copy-start.1 = (bf16[50,100,128]{2,1,0:T(8,128)(2,1)S(1)}, bf16[50,100,128]{2,1,0:T(8,128)(2,1)}, u32[]{:S(2)}) copy-start(bf16[50,100,128]{2,1,0:T(8,128)(2,1)} %v_ref.1) | copy-start | bytes 3840004
  83.6 9.5 %collective-permute-start.9 = (bf16[32,160,128]{2,1,0:T(8,128)(2,1)S(1)}, bf16[32,160,128]{2,1,0:T(8,128)(2,1)S(1)}, u32[]{:S(2)}, u32[]{:S(2)}) collective-permute-start(bf16[32,160,128]{2,1,0:T(8,128)(2,1)S(1)} %get-tuple-element.59), channel_id=1, source_target_pairs={{0,1},{1,0},{2,3},{3,2},{4,5},{5,4},{6,7},{7,6},{8,9},{9,8},{10,11... | collective-permute-start | bytes 3932168 | tf_op jit(solution)/shard_map/ppermute | solution.py:342
